TPU v7x, 256 devices: a whole 4x4x8 slice. The times are simulated.
256 devices in a mesh: row: 8 (over x_hi, y), col: 8 (over z), fsdp: 4 (over x_lo, core).
Axes of the slice: x: 4 (x_hi: 2, x_lo: 2; x = x_hi * 2 + x_lo), y: 4, z: 8, core: 2. Of those that a mesh axis runs over, the one named last changes fastest.
Arguments:
- tokens: bfloat16 [4, 64, 128, 6144], P('fsdp', 'row', 'col'), may hold values from -6 to 6
- ln_gain: float32 [6144], replicated, may hold values from 0.5 to 1.5
- qkv_blocks: bfloat16 [72, 6, 128, 128], P('fsdp'), may hold values from -0.21875 to 0.21875
- qkv_index: int32 [72, 6], replicated, may hold values from 0 to 47, as said below
- out_blocks: bfloat16 [48, 3, 128, 128], P('fsdp'), may hold values from -0.3125 to 0.3125
- out_index: int32 [48, 3], replicated, may hold values from 0 to 23, as said below
- rel_bias: float32 [24, 81], replicated, may hold values from -2 to 2
Outputs:
- mixed: bfloat16 [4, 64, 128, 6144], P('fsdp', 'row', 'col')
Inputs may be any that keep to these rules, and one draw needn't show every extreme that they name: `qkv_index`: each row names 6 different row blocks in increasing order. `out_index`: each row names 3 different row blocks in increasing order.
All inputs are finite; a program needn't handle non-finite values.
Results may differ from a plain program's by a relative error of at most 0.0039.
Values may be sent and summed in bfloat16 or wider, within the bound.
A program may use at most 128 MiB of HBM per device.

v0:
```python
import jax
import jax.numpy as jnp
from jax import lax
from jax.sharding import PartitionSpec as P

RADIUS = 4


def with_halo(x, sides, width):
    for axis, dim in sides:
        size, length = (lax.axis_size(axis), x.shape[dim])
        up = [(i, (i + 1) % size) for i in range(size - 1)]
        down = [(j, i) for i, j in up]
        last = lax.slice_in_dim(x, length - width, length, axis=dim)
        leading = lax.slice_in_dim(x, 0, width, axis=dim)
        before = lax.ppermute(last, axis, up)
        after = lax.ppermute(leading, axis, down)
        x = jnp.concatenate([before, x, after], axis=dim)
    return x


def block_product(rows_in, blocks, block_ids):
    count = rows_in.shape[0]
    head_size = blocks.shape[2]
    blocks_of = rows_in.reshape(count, -1, head_size)
    picked = jnp.take(blocks_of, block_ids, axis=1)
    result = jnp.einsum("tnkd,nkde->tne", picked, blocks, preferred_element_type=jnp.float32)
    return result.reshape(count, -1)


def neighbourhood(query, kv_rim, bias, row_first, col_first, height, width):
    tile_rows, tile_cols, channels = query.shape
    head_count = bias.shape[0]
    head_size = channels // head_count
    window = 2 * RADIUS + 1
    rim_cols = tile_cols + 2 * RADIUS
    score_scale = 1.0 / jnp.sqrt(jnp.float32(head_size))
    query_heads = query.reshape(tile_rows, tile_cols, head_count, head_size)
    col_query = jnp.arange(tile_cols, dtype=jnp.int32)[:, None]
    col_key = jnp.arange(rim_cols, dtype=jnp.int32)[None, :]
    shift_of = col_key - col_query
    in_band = (shift_of >= 0) & (shift_of < window)
    onehot = (shift_of[:, :, None] == jnp.arange(window, dtype=jnp.int32)[None, None, :]).astype(
        jnp.float32
    )
    bias_square = bias.reshape(head_count, window, window)
    bias_band = jnp.einsum("hrb,xcb->hxrc", bias_square, onehot, precision=lax.Precision.HIGHEST)
    key_col_pos = col_first + col_key - RADIUS
    col_inside = in_band & (key_col_pos >= 0) & (key_col_pos < width)
    rim_rows = jnp.arange(window, dtype=jnp.int32)

    def one_row(row_at):
        rim_slab = lax.dynamic_slice(
            kv_rim, (row_at, jnp.int32(0), jnp.int32(0)), (window, rim_cols, 2 * channels)
        )
        key_slab = rim_slab[:, :, :channels].reshape(window, rim_cols, head_count, head_size)
        value_slab = rim_slab[:, :, channels:].reshape(window, rim_cols, head_count, head_size)
        logits = jnp.einsum(
            "xhd,rchd->hxrc", query_heads[row_at], key_slab, preferred_element_type=jnp.float32
        )
        logits = logits * score_scale + bias_band
        key_row_pos = row_first + row_at + rim_rows - RADIUS
        row_inside = (key_row_pos >= 0) & (key_row_pos < height)
        allowed = row_inside[None, None, :, None] & col_inside[None, :, None, :]
        weights = jnp.where(
            allowed, jnp.exp(jnp.where(allowed, logits, jnp.float32(0.0))), jnp.float32(0.0)
        )
        denominator = jnp.sum(weights, axis=(2, 3), keepdims=True)
        prob_low = (weights / denominator).astype(jnp.bfloat16)
        summed = jnp.einsum(
            "hxrc,rchd->xhd", prob_low, value_slab, preferred_element_type=jnp.float32
        )
        return summed.astype(jnp.bfloat16).reshape(tile_cols, channels)

    return lax.map(one_row, jnp.arange(tile_rows, dtype=jnp.int32))


def body(tokens, ln_gain, qkv_blocks, qkv_index, out_blocks, out_index, rel_bias):
    tile_rows = tokens.shape[1]
    tile_cols = tokens.shape[2]
    width_all = tokens.shape[3]
    count = tile_rows * tile_cols
    widened = tokens[0].astype(jnp.float32).reshape(count, width_all)
    average = jnp.mean(widened, axis=-1, keepdims=True)
    variance = jnp.mean((widened - average) ** 2, axis=-1, keepdims=True)
    normed = ((widened - average) * lax.rsqrt(variance + 1e-06) * ln_gain).astype(jnp.bfloat16)
    block_ids = qkv_index
    projected = block_product(
        normed, lax.all_gather(qkv_blocks, "fsdp", axis=0, tiled=True), block_ids
    ).astype(jnp.bfloat16)
    channels = projected.shape[1] // 3
    projected = projected.reshape(tile_rows, tile_cols, 3 * channels)
    query = projected[:, :, :channels]
    kv_both = projected[:, :, channels:]
    kv_rim = with_halo(kv_both, (("row", 0), ("col", 1)), RADIUS)
    row_first = lax.axis_index("row") * tile_rows
    col_first = lax.axis_index("col") * tile_cols
    height = tile_rows * lax.axis_size("row")
    width = tile_cols * lax.axis_size("col")
    attended = neighbourhood(query, kv_rim, rel_bias, row_first, col_first, height, width)
    attended = attended.reshape(count, channels)
    block_ids = out_index
    branch = block_product(
        attended, lax.all_gather(out_blocks, "fsdp", axis=0, tiled=True), block_ids
    )
    mixed = (widened + branch).astype(jnp.bfloat16)
    return mixed.reshape(1, tile_rows, tile_cols, width_all)


def solution(mesh):
    in_specs = (
        P("fsdp", "row", "col", None),
        P(),
        P("fsdp", None, None, None),
        P(),
        P("fsdp", None, None, None),
        P(),
        P(),
    )
    out_specs = P("fsdp", "row", "col", None)
    return jax.shard_map(body, mesh=mesh, in_specs=in_specs, out_specs=out_specs, check_vma=False)
```

profile of v0, /device:TPU:101, one launch (start us, length us, event | category | flops | bytes accessed | tf_op | source)
XLA Modules:
  0.0 357.7 jit_solution(4510379274005370273)
XLA Ops:
  11.4 3.1 fusion.35
  14.5 13.5 %gather_fusion = bf16[432,128,128]{2,1,0:T(8,128)(2,1)} fusion(bf16[128,48,128]{2,0,1:T(8,128)(2,1)S(1)} %fusion.35, s32[1024]{0:T(1024)S(1)} %pad_clamp_fusion.1), kind=kCustom, calls=%fused_computation | custom fusion | bytes 28313280 | tf_op jit(solution)/shard_map/jit(_take)/gather | solution.py:26
  28.0 115.0 %all-gather.3.cloned.1.call-done = bf16[72,6,128,128]{3,2,1,0:T(8,128)(2,1)} async-done(((bf16[18,6,128,128]{3,2,1,0:T(8,128)(2,1)}), bf16[72,6,128,128]{3,2,1,0:T(8,128)(2,1)}) %all-gather.3.cloned.1.call-update) | async-done | bytes 14155792 | tf_op jit(solution)/shard_map/all_gather | solution.py:89
  143.0 11.1 %fusion.36 = bf16[128,72,128]{2,0,1:T(8,128)(2,1)S(1)} fusion(bf16[72,6,128,128]{3,2,1,0:T(8,128)(2,1)} %all-gather.3.cloned.1.call-done, bf16[72,6,128,128]{3,2,1,0:T(8,128)(2,1)} %bitcast.99, pred[72,6]{1,0:T(8,128)(4,1)S(1)} %copy.44), kind=kOutput, calls=%fused_computation.46 | convolution fusion | flops 1820196864 | bytes 30671280 | tf_op jit(solution)/shard_map/tnkd,nkde->tne/dot_general | solution.py:27
  161.5 3.1 collective-permute-start
  164.7 5.8 %collective-permute-start.1 = (bf16[4,16,6144]{2,1,0:T(8,128)(2,1)}, bf16[4,16,6144]{2,1,0:T(8,128)(2,1)}, u32[]{:S(2)}, u32[]{:S(2)}) collective-permute-start(bf16[4,16,6144]{2,1,0:T(8,128)(2,1)} %get-tuple-element.203), channel_id=1, source_target_pairs={{32,0},{64,32},{96,64},{128,96},{160,128},{192,160},{224,192},{33,... | collective-permute-start | bytes 2359304 | tf_op jit(solution)/shard_map/ppermute | solution.py:17
  170.7 15.1 %collective-permute-done = bf16[4,16,6144]{2,1,0:T(8,128)(2,1)S(1)} collective-permute-done((bf16[4,16,6144]{2,1,0:T(8,128)(2,1)}, bf16[4,16,6144]{2,1,0:T(8,128)(2,1)S(1)}, u32[]{:S(2)}, u32[]{:S(2)}) %collective-permute-start) | collective-permute-done | bytes 786464 | tf_op jit(solution)/shard_map/ppermute | solution.py:16
  185.8 6.5 %collective-permute-done.1 = bf16[4,16,6144]{2,1,0:T(8,128)(2,1)} collective-permute-done((bf16[4,16,6144]{2,1,0:T(8,128)(2,1)}, bf16[4,16,6144]{2,1,0:T(8,128)(2,1)}, u32[]{:S(2)}, u32[]{:S(2)}) %collective-permute-start.1) | collective-permute-done | bytes 786464 | tf_op jit(solution)/shard_map/ppermute | solution.py:17
  195.0 4.5 %collective-permute-start.2 = (bf16[16,4,6144]{2,1,0:T(4,128)(2,1)}, bf16[16,4,6144]{2,1,0:T(4,128)(2,1)}, u32[]{:S(2)}, u32[]{:S(2)}) collective-permute-start(bf16[16,4,6144]{2,1,0:T(4,128)(2,1)} %get-tuple-element.200), channel_id=1, source_target_pairs={{0,4},{4,8},{8,12},{12,16},{16,20},{20,24},{24,28},{1,5},{5,9},{9,... | collective-permute-start | bytes 2359304 | tf_op jit(solution)/shard_map/ppermute | solution.py:16
  207.3 9.7 %collective-permute-done.2 = bf16[16,4,6144]{2,1,0:T(4,128)(2,1)} collective-permute-done((bf16[16,4,6144]{2,1,0:T(4,128)(2,1)}, bf16[16,4,6144]{2,1,0:T(4,128)(2,1)}, u32[]{:S(2)}, u32[]{:S(2)}) %collective-permute-start.2) | collective-permute-done | bytes 786464 | tf_op jit(solution)/shard_map/ppermute | solution.py:16
  217.0 5.5 %collective-permute-done.3 = bf16[16,4,6144]{2,1,0:T(4,128)(2,1)} collective-permute-done((bf16[16,4,6144]{2,1,0:T(4,128)(2,1)}, bf16[16,4,6144]{2,1,0:T(4,128)(2,1)}, u32[]{:S(2)}, u32[]{:S(2)}) %collective-permute-start.3) | collective-permute-done | bytes 786464 | tf_op jit(solution)/shard_map/ppermute | solution.py:17
  222.5 5.7 %pad_maximum_fusion = bf16[16,24,6144]{2,1,0:T(8,128)(2,1)} fusion(bf16[16,4,6144]{2,1,0:T(4,128)(2,1)} %collective-permute-done.3, bf16[4,16,6144]{2,1,0:T(8,128)(2,1)} %collective-permute-done.1, bf16[8,16,6144]{2,1,0:T(8,128)(2,1)S(1)} %copy-done.5, bf16[4,16,6144]{2,1,0:T(8,128)(2,1)S(1)} %collective-permute-done, ...), kind=kLoop, calls=%fused_computation.34 | loop fusion | flops 23592960 | bytes 9437184 | tf_op jit(solution)/shard_map/concatenate | solution.py:18
  228.2 97.2 %while.13 = (s32[]{:T(128)}, bf16[8,16,3072]{2,1,0:T(8,128)(2,1)}, s32[8]{0:T(128)S(1)}, bf16[16,24,6144]{2,1,0:T(8,128)(2,1)}, s32[]{:T(128)}, /*index=5*/bf16[...) while((s32[]{:T(128)}, bf16[8,16,3072]{2,1,0:T(8,128)(2,1)}, ...), condition=%wide.region_4.5_spmd.clone, body=%wide.region_2.0_spmd.clone.sunk | while | flops 43102516 | bytes 15261010 | solution.py:75
  242.9 3.0 dynamic-slice_bitcast_fusion.3
  255.0 3.0 dynamic-slice_bitcast_fusion.3
  267.2 3.0 dynamic-slice_bitcast_fusion.3
  291.5 3.0 dynamic-slice_bitcast_fusion.3
  303.6 3.0 dynamic-slice_bitcast_fusion.3
  315.8 3.0 dynamic-slice_bitcast_fusion.3
  326.9 7.6 %gather_fusion.1 = bf16[144,128,128]{2,1,0:T(8,128)(2,1)} fusion(bf16[128,24,128]{2,0,1:T(8,128)(2,1)S(1)} %copy.52, s32[1024]{0:T(1024)S(1)} %pad_clamp_fusion), kind=kCustom, calls=%fused_computation.1 | custom fusion | bytes 9437760 | tf_op jit(solution)/shard_map/jit(_take)/gather | solution.py:26
  334.5 5.2 %fusion.40 = f32[128,48,128]{2,0,1:T(8,128)S(1)} fusion(bf16[48,3,128,128]{3,2,1,0:T(8,128)(2,1)} %all-gather.5.cloned.1.call-done, bf16[48,3,128,128]{3,2,1,0:T(8,128)(2,1)} %bitcast.103, pred[48,3]{1,0:T(8,128)(4,1)S(1)} %copy.43), kind=kOutput, calls=%fused_computation.49 | convolution fusion | flops 606339072 | bytes 12583056 | tf_op jit(solution)/shard_map/tnkd,nkde->tne/dot_general | solution.py:27
  339.7 3.5 copy.53
  343.2 4.4 %reshape.138 = f32[1,8,16,6144]{3,2,1,0:T(8,128)} reshape(f32[128,48,128]{2,1,0:T(8,128)} %copy.53) | data formatting | bytes 6291456 | tf_op jit(solution)/shard_map/reshape | solution.py:28
  347.6 3.3 add_convert_fusion
  (159 shorter events, 72.8 us)
Async XLA Ops:
  6.5 1.4 copy-start.1
  6.5 136.5 %all-gather.3.cloned.1.call-start = ((), (), s32[]{:S(2)}) async-start(), calls=%async_computation | async-start | bytes 17694720 | tf_op jit(solution)/shard_map/all_gather | solution.py:89
  7.3 327.2 %all-gather.5.cloned.1.call-start = ((), (), s32[]{:S(2)}) async-start(), calls=%async_computation.1 | async-start | bytes 5898240 | tf_op jit(solution)/shard_map/all_gather | solution.py:104
  8.3 2.7 copy-start.7
  8.3 3.0 copy-start.6
  160.1 10.6 %copy-start.3 = (bf16[8,16,9216]{2,1,0:T(8,128)(2,1)}, bf16[8,16,9216]{2,1,0:T(8,128)(2,1)S(1)}, u32[]{:S(2)}) copy-start(bf16[8,16,9216]{2,1,0:T(8,128)(2,1)S(1)} %convert_element_type.53) | copy-start | bytes 7077892
  160.1 10.4 %copy-start.8 = (f32[24,81]{1,0:T(8,128)S(1)}, f32[24,81]{1,0:T(8,128)}, u32[]{:S(2)}) copy-start(f32[24,81]{1,0:T(8,128)} %param.15) | copy-start | bytes 23332
  161.5 24.3 %collective-permute-start = (bf16[4,16,6144]{2,1,0:T(8,128)(2,1)}, bf16[4,16,6144]{2,1,0:T(8,128)(2,1)S(1)}, u32[]{:S(2)}, u32[]{:S(2)}) collective-permute-start(bf16[4,16,6144]{2,1,0:T(8,128)(2,1)} %get-tuple-element.202), channel_id=1, source_target_pairs={{0,32},{32,64},{64,96},{96,128},{128,160},{160,192},{192,224},{1,3... | collective-permute-start | bytes 2359304 | tf_op jit(solution)/shard_map/ppermute | solution.py:16
  164.7 27.6 %collective-permute-start.1 = (bf16[4,16,6144]{2,1,0:T(8,128)(2,1)}, bf16[4,16,6144]{2,1,0:T(8,128)(2,1)}, u32[]{:S(2)}, u32[]{:S(2)}) collective-permute-start(bf16[4,16,6144]{2,1,0:T(8,128)(2,1)} %get-tuple-element.203), channel_id=1, source_target_pairs={{32,0},{64,32},{96,64},{128,96},{160,128},{192,160},{224,192},{33,... | collective-permute-start | bytes 2359304 | tf_op jit(solution)/shard_map/ppermute | solution.py:17
  170.7 33.2 %copy-start.4 = (bf16[8,16,6144]{2,1,0:T(8,128)(2,1)}, bf16[8,16,6144]{2,1,0:T(8,128)(2,1)S(1)}, u32[]{:S(2)}) copy-start(bf16[8,16,6144]{2,1,0:T(8,128)(2,1)S(1)} %slice.45) | copy-start | bytes 4718596
  195.0 10.9 %copy-start.9 = (s32[48,3]{0,1:T(4,128)S(1)}, s32[48,3]{0,1:T(4,128)}, u32[]{:S(2)}) copy-start(s32[48,3]{0,1:T(4,128)} %param.14) | copy-start | bytes 1732
  195.0 22.0 %collective-permute-start.2 = (bf16[16,4,6144]{2,1,0:T(4,128)(2,1)}, bf16[16,4,6144]{2,1,0:T(4,128)(2,1)}, u32[]{:S(2)}, u32[]{:S(2)}) collective-permute-start(bf16[16,4,6144]{2,1,0:T(4,128)(2,1)} %get-tuple-element.200), channel_id=1, source_target_pairs={{0,4},{4,8},{8,12},{12,16},{16,20},{20,24},{24,28},{1,5},{5,9},{9,... | collective-permute-start | bytes 2359304 | tf_op jit(solution)/shard_map/ppermute | solution.py:16
  199.5 6.7 %slice-start = ((bf16[8,16,9216]{2,1,0:T(8,128)(2,1)}), bf16[8,16,3072]{2,1,0:T(8,128)(2,1)S(1)}, s32[]{:S(2)}) async-start(bf16[8,16,9216]{2,1,0:T(8,128)(2,1)} %copy-done.3), calls=%async_computation.2 | async-start | bytes 1572864 | tf_op jit(solution)/shard_map/slice | solution.py:93
  199.5 23.0 %collective-permute-start.3 = (bf16[16,4,6144]{2,1,0:T(4,128)(2,1)}, bf16[16,4,6144]{2,1,0:T(4,128)(2,1)}, u32[]{:S(2)}, u32[]{:S(2)}) collective-permute-start(bf16[16,4,6144]{2,1,0:T(4,128)(2,1)} %get-tuple-element.201), channel_id=1, source_target_pairs={{4,0},{8,4},{12,8},{16,12},{20,16},{24,20},{28,24},{5,1},{9,5},{13... | collective-permute-start | bytes 2359304 | tf_op jit(solution)/shard_map/ppermute | solution.py:17
  206.2 16.3 %copy-start.5 = (bf16[8,16,6144]{2,1,0:T(8,128)(2,1)S(1)}, bf16[8,16,6144]{2,1,0:T(8,128)(2,1)}, u32[]{:S(2)}) copy-start(bf16[8,16,6144]{2,1,0:T(8,128)(2,1)} %copy-done.4) | copy-start | bytes 4718596
  236.5 2.4 copy-start
  248.6 2.4 copy-start
  260.8 2.4 copy-start
  272.9 2.4 copy-start
  285.1 2.4 copy-start
  297.3 2.4 copy-start
  309.4 2.4 copy-start
  321.6 2.4 copy-start
  343.2 4.4 %copy-start.2 = (bf16[1,8,16,6144]{3,2,1,0:T(8,128)(2,1)S(1)}, bf16[1,8,16,6144]{3,2,1,0:T(8,128)(2,1)}, u32[]{:S(2)}) copy-start(bf16[1,8,16,6144]{3,2,1,0:T(8,128)(2,1)} %param.9) | copy-start | bytes 4718596
Sparse Core Ops, SparseCore 0:
  9.2 133.8 all-gather.2
  170.6 56.5 all-gather.4
where the time goes:
time: 362 us; the launch traced here: 358 us
  waiting for transfers between devices  153 us (42%)
  local copies, waits for them, and re-layouts  86 us (24%)
  matrix products  42.6 us (12%)
  loops' own time  30.8 us (9%)
  other arithmetic  16.5 us (5%)
  starting transfers between devices  15.7 us (4%)
  between operations  13.6 us (4%)
    all_gather x1, waiting for transfers between devices, body(): lax.all_gather(qkv_blocks, 'fsdp', axis=0, tiled=True)  115 us
    another operation x1, loops' own time, neighbourhood(): return lax.map(one_row, jnp.arange(tile_rows, dtype=jnp.int32))  30.8 us
    ppermute x2, waiting for transfers between devices, with_halo(): before = lax.ppermute(last, axis, up)  24.8 us
    while x24, local copies, waits for them, and re-layouts  23.7 us
    gather x2, local copies, waits for them, and re-layouts, block_product(): picked = jnp.take(blocks_of, block_ids, axis=1)  21.1 us
    dot_general x8, matrix products, one_row(): jnp.einsum('xhd,rchd->hxrc', query_heads[row_at], key_slab, preferred_ele...  17.8 us
    dot_general x2, matrix products, block_product(): jnp.einsum('tnkd,nkde->tne', picked, blocks, preferred_element_type=jnp.f...  16.4 us
    ppermute x2, waiting for transfers between devices, with_halo(): after = lax.ppermute(leading, axis, down)  12 us
  transfers between devices with their start and end apart: 6, of which 5 were waited for; matrix products, arithmetic and copies ran while one was open for 31% of the time, Pallas kernels for 0%

commit v1 on v0

v1 whole, which is shorter than its diff:
```python
import functools

import jax
import jax.numpy as jnp
from jax import lax
from jax.experimental import pallas as pl
from jax.experimental.pallas import tpu as pltpu
from jax.sharding import PartitionSpec as P

MESH = pl.DeviceIdType.MESH
HD = 128
HEADS = 24
KEEP = 6
KEEP_O = 3
RADIUS = 4
TH, TW = 8, 16
OWN = TH * TW
ALL = (TH + 2 * RADIUS) * (TW + 2 * RADIUS)
GROUPS = 48
SHARD = 18
SHARD_O = 12
NEG = -1e30
SLOT = dict(S=(128, 64), N=(192, 64), NW=(256, 16), W=(272, 32), SW=(304, 16), NE=(320, 16), E=(336, 32), SE=(368, 16))
SIDES = dict(S=(1, 0), N=(-1, 0), NW=(-1, -1), W=(0, -1), SW=(1, -1), NE=(-1, 1), E=(0, 1), SE=(1, 1))
OPPOSITE = dict(S="N", N="S", NW="SE", SE="NW", NE="SW", SW="NE", W="E", E="W")
NAMES = tuple(SLOT)
X_CB = 12
Z_CB = 6


def kernel(
    qi, oi, tok, left, right, gain, base, wq, wo, out,
    T, N, W, WO, QKV, ATT, B,
    loc, hs, hr, xs, xr, zs, zr, ss, sr, bxs, bxr, bys, byr, bss, bsr,
):
    row, col, fs_ = lax.axis_index("row"), lax.axis_index("col"), lax.axis_index("fsdp")
    x, y, z, k = (row // 4) * 2 + fs_ // 2, row % 4, col, fs_ % 2

    def dev(dx, dy, dz, dk):
        xx, yy, zz, kk = (x + dx) % 4, (y + dy) % 4, (z + dz) % 8, (k + dk) % 2
        return ((xx // 2) * 4 + yy, zz, (xx % 2) * 2 + kk)

    def tile(dr, dc):
        return ((row + dr + 8) % 8, (col + dc + 8) % 8, fs_)

    f_own = fs_
    f_sib = (x % 2) * 2 + (1 - k)
    f_oth = (1 - x % 2) * 2 + k
    f_osb = (1 - x % 2) * 2 + (1 - k)
    cz, cy = z % 2, y % 2
    sib = dev(0, 0, 0, 1)
    xp, xm = dev(1, 0, 0, 0), dev(3, 0, 0, 0)
    yp, ym = dev(0, 1, 0, 0), dev(0, 3, 0, 0)
    zp, zm = dev(0, 0, 1, 0), dev(0, 0, 7, 0)

    def acb(i, color):
        return i + color * (SHARD - 1 - 2 * i)

    c_tok = pltpu.make_async_copy(tok, T.at[pl.ds(0, OWN)], loc.at[0])
    c_wq = pltpu.make_async_copy(wq, W.at[pl.ds(f_own * 108, 108)], loc.at[1])
    c_wo = pltpu.make_async_copy(wo, WO.at[pl.ds(f_own * 36, 36)], loc.at[2])
    c_tok.start()
    c_wq.start()
    c_wo.start()

    partners = [sib, xp, xm, yp, ym, zp, zm, tile(1, 0), tile(-1, 0), tile(1, 1), tile(1, -1), tile(-1, 1), tile(-1, -1)]
    barrier = pltpu.get_barrier_semaphore()
    for p in partners:
        pl.semaphore_signal(barrier, inc=1, device_id=p, device_id_type=MESH)
    pl.semaphore_wait(barrier, len(partners))

    def rc(src, dst, s, r, to):
        return pltpu.make_async_remote_copy(src_ref=src, dst_ref=dst, send_sem=s, recv_sem=r, device_id=to, device_id_type=MESH)

    def cols(f, cb):
        return W.at[pl.ds((f * SHARD + cb) * KEEP, KEEP)]

    def x_send(i):
        cb = acb(i, cz)
        return rc(wq.at[pl.ds(cb * KEEP, KEEP)], cols(f_own, cb), xs.at[i], xr.at[i], xp if (i // 3) % 2 == 0 else xm)

    def x_recv(i):
        d = cols(f_oth, acb(i, cz))
        return rc(d, d, xs.at[i], xr.at[i], xp)

    def z_send(i):
        d = cols(f_oth, acb(i, cz))
        return rc(d, d, zs.at[i], zr.at[i], zp if i < 3 else zm)

    def z_recv(i):
        d = cols(f_oth, acb(i, 1 - cz))
        return rc(d, d, zs.at[i], zr.at[i], zp)

    def s_send(i):
        d = cols(f_oth, acb(i, cz) if i < X_CB else acb(i - X_CB, 1 - cz))
        return rc(d, d, ss.at[i], sr.at[i], sib)

    def s_recv(i):
        d = cols(f_osb, acb(i, cz) if i < X_CB else acb(i - X_CB, 1 - cz))
        return rc(d, d, ss.at[i], sr.at[i], sib)

    def o_cols(f, part):
        return WO.at[pl.ds(f * 36 + part * 9, 9)]

    def bx_send(i):
        part = cy * 2 + i
        return rc(wo.at[pl.ds(part * 9, 9)], o_cols(f_own, part), bxs.at[i], bxr.at[i], xp if i == 0 else xm)

    def bx_recv(i):
        d = o_cols(f_oth, cy * 2 + i)
        return rc(d, d, bxs.at[i], bxr.at[i], xp)

    def by_send(i):
        d = o_cols(f_oth, cy * 2 + i)
        return rc(d, d, bys.at[i], byr.at[i], yp if i == 0 else ym)

    def by_recv(i):
        d = o_cols(f_oth, (1 - cy) * 2 + i)
        return rc(d, d, bys.at[i], byr.at[i], yp)

    def bs_send(i):
        d = o_cols(f_oth, cy * 2 + i if i < 2 else (1 - cy) * 2 + i - 2)
        return rc(d, d, bss.at[i], bsr.at[i], sib)

    def bs_recv(i):
        d = o_cols(f_osb, cy * 2 + i if i < 2 else (1 - cy) * 2 + i - 2)
        return rc(d, d, bss.at[i], bsr.at[i], sib)

    sa_send = rc(wq, W.at[pl.ds(f_own * 108, 108)], ss.at[18], sr.at[18], sib)
    d_sa = W.at[pl.ds(f_sib * 108, 108)]
    sa_recv = rc(d_sa, d_sa, ss.at[18], sr.at[18], sib)
    sb_send = rc(wo, WO.at[pl.ds(f_own * 36, 36)], bss.at[4], bsr.at[4], sib)
    d_sb = WO.at[pl.ds(f_sib * 36, 36)]
    sb_recv = rc(d_sb, d_sb, bss.at[4], bsr.at[4], sib)

    def exists(name):
        dr, dc = SIDES[name]
        cond = row >= 0
        if dr < 0:
            cond = row > 0
        if dr > 0:
            cond = row < 7
        if dc < 0:
            cond = cond & (col > 0)
        if dc > 0:
            cond = cond & (col < 7)
        return cond

    src_of = dict(
        S=tok.at[pl.ds(64, 64)], N=tok.at[pl.ds(0, 64)], W=left, E=right,
        NW=left.at[pl.ds(0, 16)], SW=left.at[pl.ds(16, 16)], NE=right.at[pl.ds(0, 16)], SE=right.at[pl.ds(16, 16)],
    )

    def h_send(name):
        slot = OPPOSITE[name]
        j = NAMES.index(slot)
        return rc(src_of[name], T.at[pl.ds(*SLOT[slot])], hs.at[j], hr.at[j], tile(*SIDES[name]))

    def h_recv(name):
        j = NAMES.index(name)
        d = T.at[pl.ds(*SLOT[name])]
        return rc(d, d, hs.at[j], hr.at[j], sib)

    x_sends = [x_send(i) for i in range(X_CB)]
    for i in (0, 3, 1, 4, 2, 5):
        x_sends[i].start()
    for name in ("E", "W", "S", "N", "NW", "NE", "SW", "SE"):
        @pl.when(exists(name))
        def _():
            h_send(name).start()
    sa_send.start()
    for i in (6, 9, 7, 10, 8, 11):
        x_sends[i].start()

    def layernorm(first, count):
        def step(g, _):
            r = pl.multiple_of(first + g * 16, 16)
            v = T[pl.ds(r, 16), :].astype(jnp.float32)
            mean = jnp.sum(v, axis=1, keepdims=True) * (1.0 / 6144)
            d = v - mean
            var = jnp.sum(d * d, axis=1, keepdims=True) * (1.0 / 6144)
            n = (d * lax.rsqrt(var + 1e-06) * gain[...]).astype(jnp.bfloat16)
            for j in range(GROUPS):
                N[j, pl.ds(r, 16), :] = n[:, j * HD : (j + 1) * HD]
            return 0

        lax.fori_loop(0, count // 16, step, 0)

    def project(cb, r0, nr):
        lhs = jnp.concatenate([N[qi[cb, j], r0 : r0 + nr, :] for j in range(KEEP)], axis=1)
        w = W[pl.ds(cb * KEEP, KEEP)].reshape(KEEP * HD, HD)
        acc = jnp.dot(lhs, w, preferred_element_type=jnp.float32)
        QKV[cb, r0 : r0 + nr, :] = acc.astype(jnp.bfloat16)

    def project_range(lo, hi, r0, nr):
        def step(cb, _):
            project(cb, r0, nr)
            return 0

        lax.fori_loop(lo, hi, step, 0)

    def make_bias():
        i_q = lax.broadcasted_iota(jnp.int32, (8, ALL), 0)
        lane = lax.broadcasted_iota(jnp.int32, (8, ALL), 1)
        mid = lane < 256
        gy = lane // 16
        side = lane - 256
        side_y = (side % 64) // 4 - 4
        side_x = side % 4 + jnp.where(side < 64, -4, 16)
        ky = jnp.where(mid, jnp.where(gy >= 12, gy - 16, gy), side_y)
        kx = jnp.where(mid, lane % 16, side_x)
        gky, gkx = ky + row * TH, kx + col * TW
        inside = (gky >= 0) & (gky < 8 * TH) & (gkx >= 0) & (gkx < 8 * TW)
        for g in range(OWN // 8):
            qy, qx = g // 2, (g % 2) * 8 + i_q
            ok = inside & (jnp.abs(ky - qy) <= RADIUS) & (jnp.abs(kx - qx) <= RADIUS)

            def step(h, _):
                b = jnp.broadcast_to(base[pl.ds(h, 1), :], (8, 512))
                m = pltpu.roll(pltpu.roll(b[:, :256], (8 * g - 68) % 256, 1), 0, 1, stride=1, stride_axis=0)
                if g % 2 == 0:
                    s = pltpu.roll(b[:, 256:384], 4 * qy, 1, stride=1, stride_axis=0)
                else:
                    s = pltpu.roll(b[:, 384:512], 57 + 4 * qy, 1, stride=1, stride_axis=0)
                B[h, 8 * g : 8 * g + 8, :] = jnp.where(ok, jnp.concatenate([m, s], axis=1), NEG)
                return 0

            lax.fori_loop(0, HEADS, step, 0)

    def attend(h):
        q = QKV[h, 0:OWN, :]
        s = lax.dot_general(q, QKV[HEADS + h], (((1,), (1,)), ((), ())), preferred_element_type=jnp.float32)
        s = s * (HD ** -0.5) + B[h]
        m = jnp.max(s, axis=1, keepdims=True)
        p = jnp.exp(s - m)
        total = jnp.sum(p, axis=1, keepdims=True)
        o = jnp.dot(p.astype(jnp.bfloat16), QKV[2 * HEADS + h], preferred_element_type=jnp.float32)
        ATT[h] = (o / total).astype(jnp.bfloat16)

    def output(cb):
        lhs = jnp.concatenate([ATT[oi[cb, j]] for j in range(KEEP_O)], axis=1)
        w = WO[pl.ds(cb * KEEP_O, KEEP_O)].reshape(KEEP_O * HD, HD)
        acc = jnp.dot(lhs, w, preferred_element_type=jnp.float32)
        lanes = pl.ds(pl.multiple_of(cb * HD, HD), HD)
        out[:, lanes] = (acc + T[0:OWN, lanes].astype(jnp.float32)).astype(jnp.bfloat16)

    c_tok.wait()
    layernorm(0, OWN)
    for i in (0, 3):
        x_recv(i).wait_recv()
        z_send(i).start()
        s_send(i).start()
    make_bias()
    for i in (1, 4, 2, 5):
        x_recv(i).wait_recv()
        z_send(i).start()
        s_send(i).start()
    c_wq.wait()
    project_range(f_own * SHARD, f_own * SHARD + SHARD, 0, OWN)
    sa_recv.wait_recv()
    project_range(f_sib * SHARD, f_sib * SHARD + SHARD, 0, OWN)

    for i in (6, 9, 7, 10, 8, 11):
        x_recv(i).wait_recv()
        s_send(i).start()
    bx_sends = [bx_send(i) for i in range(2)]
    for c in bx_sends:
        c.start()
    sb_send.start()

    for name in NAMES:
        first, count = SLOT[name]

        @pl.when(exists(name))
        def _():
            h_recv(name).wait_recv()

        @pl.when(jnp.logical_not(exists(name)))
        def _():
            T[first : first + count, :] = jnp.zeros((count, 6144), jnp.bfloat16)

    layernorm(OWN, ALL - OWN)

    for i in range(Z_CB):
        z_recv(i).wait_recv()
        s_send(X_CB + i).start()

    project_range(f_oth * SHARD, f_oth * SHARD + SHARD, 0, OWN)
    for i in range(2):
        bx_recv(i).wait_recv()
        by_send(i).start()
        bs_send(i).start()
    for i in range(18):
        s_recv(i).wait_recv()
    project_range(f_osb * SHARD, f_osb * SHARD + SHARD, 0, OWN)
    project_range(HEADS, 3 * HEADS, OWN, ALL - OWN)

    for i in range(2):
        by_recv(i).wait_recv()
        bs_send(2 + i).start()

    def head(h, _):
        attend(h)
        return 0

    lax.fori_loop(0, HEADS, head, 0)

    c_wo.wait()
    sb_recv.wait_recv()
    for i in range(4):
        bs_recv(i).wait_recv()

    def column(cb, _):
        output(cb)
        return 0

    lax.fori_loop(0, GROUPS, column, 0)

    for c in x_sends + bx_sends + [sa_send, sb_send]:
        c.wait_send()
    for i in range(Z_CB):
        z_send(i).wait_send()
    for i in range(18):
        s_send(i).wait_send()
    for i in range(2):
        by_send(i).wait_send()
    for i in range(4):
        bs_send(i).wait_send()
    for name in NAMES:
        @pl.when(exists(name))
        def _():
            h_send(name).wait_send()


def body(tokens, ln_gain, qkv_blocks, qkv_index, out_blocks, out_index, rel_bias):
    tile = tokens[0]
    left = tile[:, :RADIUS].reshape(TH * RADIUS, -1)
    right = tile[:, TW - RADIUS :].reshape(TH * RADIUS, -1)
    square = rel_bias.reshape(HEADS, 9, 9)
    mid = jnp.pad(square, ((0, 0), (0, 0), (0, 7))).reshape(HEADS, 144)
    mid = jnp.pad(mid, ((0, 0), (0, 112)))
    west = jnp.pad(square[:, :, :4].reshape(HEADS, 36), ((0, 0), (0, 92)))
    east = jnp.pad(square[:, :, 5:].reshape(HEADS, 36), ((0, 0), (0, 92)))
    base = jnp.concatenate([mid, west, east], axis=1)
    any_, vmem, smem = pl.BlockSpec(memory_space=pl.ANY), pl.BlockSpec(memory_space=pltpu.VMEM), pl.BlockSpec(memory_space=pltpu.SMEM)
    dma = lambda n: pltpu.SemaphoreType.DMA((n,))
    bf = jnp.bfloat16
    mixed = pl.pallas_call(
        kernel,
        out_shape=jax.ShapeDtypeStruct((OWN, 6144), bf),
        in_specs=[smem, smem, any_, any_, any_, vmem, vmem, any_, any_],
        out_specs=vmem,
        scratch_shapes=[
            pltpu.VMEM((ALL, 6144), bf),
            pltpu.VMEM((GROUPS, ALL, HD), bf),
            pltpu.VMEM((432, HD, HD), bf),
            pltpu.VMEM((144, HD, HD), bf),
            pltpu.VMEM((72, ALL, HD), bf),
            pltpu.VMEM((HEADS, OWN, HD), bf),
            pltpu.VMEM((HEADS, OWN, ALL), jnp.float32),
            dma(3), dma(8), dma(8), dma(12), dma(12), dma(6), dma(6), dma(19), dma(19),
            dma(2), dma(2), dma(2), dma(2), dma(5), dma(5),
        ],
        compiler_params=pltpu.CompilerParams(collective_id=0, has_side_effects=True, vmem_limit_bytes=58 * 2**20),
        cost_estimate=pl.CostEstimate(flops=6 * 10**9, bytes_accessed=30 * 2**20, transcendentals=10**6),
        name="block",
    )(
        qkv_index, out_index, tile.reshape(OWN, -1), left, right, ln_gain.reshape(1, -1), base,
        qkv_blocks.reshape(SHARD * KEEP, HD, HD), out_blocks.reshape(SHARD_O * KEEP_O, HD, HD),
    )
    return mixed.reshape(1, TH, TW, -1)


def solution(mesh):
    in_specs = (
        P("fsdp", "row", "col", None),
        P(),
        P("fsdp", None, None, None),
        P(),
        P("fsdp", None, None, None),
        P(),
        P(),
    )
    out_specs = P("fsdp", "row", "col", None)
    return jax.shard_map(body, mesh=mesh, in_specs=in_specs, out_specs=out_specs, check_vma=False)
```

time: 362 us -> 140 us (0.39)
  the two profiles are of different devices: /device:TPU:101 before, /device:TPU:1 now
where the time goes in v1:
time: 140 us
  Pallas kernels  129 us (92%)
  local copies, waits for them, and re-layouts  9.96 us (7%)
    pallas_call x1, Pallas kernels, body(): pl.pallas_call(kernel, out_shape=jax.ShapeDtypeStruct((OWN, 6144), bf), i...  129 us
    unnamed x4, local copies, waits for them, and re-layouts  6.25 us

profile of v1, /device:TPU:1, one launch (start us, length us, event | category | flops | bytes accessed | tf_op | source)
XLA Modules:
  0.0 139.6 jit_solution(4094649365859736281)
XLA Ops:
  0.0 1.4 copy.15.oi
  1.4 1.4 copy.14.qi
  2.8 0.8 copy.10
  3.6 0.1 copy.11
  3.7 0.1 copy.12
  3.8 0.1 copy.13
  3.9 0.6 select_maximum_fusion.base
  4.5 1.8 %fusion.1 = (bf16[8,4,6144]{2,1,0:T(4,128)(2,1)S(1)}, bf16[8,4,6144]{2,1,0:T(4,128)(2,1)S(1)}) fusion(bf16[8,16,6144]{2,1,0:T(8,128)(2,1)} %bitcast.14), kind=kLoop, calls=%fused_computation.7 | loop fusion | bytes 1572864 | tf_op jit(solution)/shard_map/slice | solution.py:338
  6.3 0.8 reshape.31.right
  7.1 0.8 reshape.30.left
  7.9 129.0 %block.1 = bf16[128,6144]{1,0:T(8,128)(2,1)} custom-call(s32[72,6]{1,0:T(8,128)} %copy.14.qi, s32[48,3]{1,0:T(8,128)} %copy.15.oi, bf16[128,6144]{1,0:T(8,128)(2,1)} %bitcast.15, bf16[32,6144]{1,0:T(8,128)(2,1)} %reshape.30.left, bf16[32,6144]{1,0:T(8,128)(2,1)} %reshape.31.right, f32[1,6144]{1,0:T(1,128)} %bitcast.19, f32[24,512]{1,0:T(8,128)} %select_maximum_fusion.base, ...), custom_call_target="tpu_custom_call" | custom-call | flops 6000000000 | bytes 31457280 | tf_op jit(solution)/shard_map/block/pallas_call | solution.py:348
  136.9 2.7 %copy.17 = bf16[1,8,16,6144]{3,2,1,0:T(8,128)(2,1)} copy(bf16[1,8,16,6144]{3,2,1,0:T(8,128)(2,1)} %bitcast.13) | data formatting | bytes 3145728
  (5 shorter events, 0.1 us)

commit v2 on v0

v2 whole, which is shorter than its diff:
```python
import jax
import jax.numpy as jnp
from jax import lax
from jax.experimental import pallas as pl
from jax.experimental.pallas import tpu as pltpu
from jax.sharding import PartitionSpec as P

MESH = pl.DeviceIdType.MESH
HD = 128
HEADS = 24
KEEP = 6
KEEP_O = 3
RADIUS = 4
TH, TW = 8, 16
OWN = TH * TW
ALL = (TH + 2 * RADIUS) * (TW + 2 * RADIUS)
PAIR = 256
GROUPS = 48
SHARD = 18
SHARD_O = 12
NEG = -1e30
STAGES = ("X1", "X2", "Y1", "Y2", "Z1", "Z2")


def kernel(
    qi, oi, tok, gain, base, wq, wo, out,
    NAT, T, N, NO, W, WO, Q, KV, ATT, B, EDGE,
    loc, hs, hr, ws, wr, ss, sr, bs, br, bss, bsr, os, orr,
):
    row, col, fs_ = lax.axis_index("row"), lax.axis_index("col"), lax.axis_index("fsdp")
    x, y, z, k = (row // 4) * 2 + fs_ // 2, row % 4, col, fs_ % 2

    def dev(dx, dy, dz, dk):
        xx, yy, zz, kk = (x + dx) % 4, (y + dy) % 4, (z + dz) % 8, (k + dk) % 2
        return ((xx // 2) * 4 + yy, zz, (xx % 2) * 2 + kk)

    def tile(dr, dc):
        return ((row + dr + 8) % 8, (col + dc + 8) % 8, fs_)

    f_own = fs_
    f_sib = (x % 2) * 2 + (1 - k)
    f_oth = (1 - x % 2) * 2 + k
    f_osb = (1 - x % 2) * 2 + (1 - k)
    cz, cy = z % 2, y % 2
    sib = dev(0, 0, 0, 1)
    xp, xm = dev(1, 0, 0, 0), dev(3, 0, 0, 0)
    yp, ym = dev(0, 1, 0, 0), dev(0, 3, 0, 0)
    zp, zm = dev(0, 0, 1, 0), dev(0, 0, 7, 0)
    chunk_of = dict(
        X1=cy, X2=2 + 2 * cy + cz, Y1=1 - cy, Y2=2 + 2 * (1 - cy) + cz, Z1=2 + 2 * cy + 1 - cz, Z2=2 + 2 * (1 - cy) + 1 - cz
    )

    c_tok = pltpu.make_async_copy(tok, NAT, loc.at[0])
    c_wq = pltpu.make_async_copy(wq, W.at[pl.ds(f_own * 108, 108)], loc.at[1])
    c_wo = pltpu.make_async_copy(wo, WO.at[pl.ds(f_own * 36, 36)], loc.at[2])
    c_tok.start()
    c_wq.start()
    c_wo.start()

    partners = [sib, xp, xm, yp, ym, zp, zm, tile(1, 0), tile(-1, 0)]
    barrier = pltpu.get_barrier_semaphore()
    for p in partners:
        pl.semaphore_signal(barrier, inc=1, device_id=p, device_id_type=MESH)
    pl.semaphore_wait(barrier, len(partners))

    def rc(src, dst, s, r, to):
        return pltpu.make_async_remote_copy(src_ref=src, dst_ref=dst, send_sem=s, recv_sem=r, device_id=to, device_id_type=MESH)

    def a_ref(f, stage, sub):
        return W.at[pl.ds(((f * 6 + chunk_of[stage]) * 3 + sub) * KEEP, KEEP)]

    def o_ref(f, stage):
        return WO.at[pl.ds((f * 6 + chunk_of[stage]) * 6, 6)]

    def a_first(stage, sub, to):
        j = STAGES.index(stage) * 3 + sub
        src = wq.at[pl.ds((chunk_of[stage] * 3 + sub) * KEEP, KEEP)]
        return rc(src, a_ref(f_own, stage, sub), ws.at[j], wr.at[j], to)

    def a_forward(have, stage, sub, to):
        j = STAGES.index(stage) * 3 + sub
        d = a_ref(f_oth, have, sub)
        return rc(d, d, ws.at[j], wr.at[j], to)

    def a_recv(stage, sub):
        j = STAGES.index(stage) * 3 + sub
        d = a_ref(f_oth, stage, sub)
        return rc(d, d, ws.at[j], wr.at[j], sib)

    def s_send(stage, sub):
        j = STAGES.index(stage) * 3 + sub
        d = a_ref(f_oth, stage, sub)
        return rc(d, d, ss.at[j], sr.at[j], sib)

    def s_recv(stage, sub):
        j = STAGES.index(stage) * 3 + sub
        d = a_ref(f_osb, stage, sub)
        return rc(d, d, ss.at[j], sr.at[j], sib)

    def o_first(stage, to):
        j = STAGES.index(stage)
        return rc(wo.at[pl.ds(chunk_of[stage] * 6, 6)], o_ref(f_own, stage), bs.at[j], br.at[j], to)

    def o_forward(have, stage, to):
        j = STAGES.index(stage)
        d = o_ref(f_oth, have)
        return rc(d, d, bs.at[j], br.at[j], to)

    def o_recv(stage):
        j = STAGES.index(stage)
        d = o_ref(f_oth, stage)
        return rc(d, d, bs.at[j], br.at[j], sib)

    def os_send(stage):
        j = STAGES.index(stage)
        d = o_ref(f_oth, stage)
        return rc(d, d, bss.at[j], bsr.at[j], sib)

    def os_recv(stage):
        j = STAGES.index(stage)
        d = o_ref(f_osb, stage)
        return rc(d, d, bss.at[j], bsr.at[j], sib)

    sa_send = rc(wq, W.at[pl.ds(f_own * 108, 108)], os.at[0], orr.at[0], sib)
    d_sa = W.at[pl.ds(f_sib * 108, 108)]
    sa_recv = rc(d_sa, d_sa, os.at[0], orr.at[0], sib)
    sb_send = rc(wo, WO.at[pl.ds(f_own * 36, 36)], os.at[1], orr.at[1], sib)
    d_sb = WO.at[pl.ds(f_sib * 36, 36)]
    sb_recv = rc(d_sb, d_sb, os.at[1], orr.at[1], sib)

    up, down, west, east = row > 0, row < 7, col > 0, col < 7
    four = pl.ds(1, 4)
    halo = dict(
        N=((four, pl.ds(32, 16)), (four, pl.ds(0, 16)), tile(1, 0), down, up),
        S=((four, pl.ds(16, 16)), (four, pl.ds(48, 16)), tile(-1, 0), up, down),
        W=((4, pl.ds(16, 32)), (0, pl.ds(16, 32)), tile(0, 1), east, west),
        E=((1, pl.ds(16, 32)), (5, pl.ds(16, 32)), tile(0, -1), west, east),
        NW=((4, pl.ds(0, 16)), (0, pl.ds(0, 16)), tile(0, 1), up & east, up & west),
        NE=((1, pl.ds(0, 16)), (5, pl.ds(0, 16)), tile(0, -1), up & west, up & east),
        SW=((4, pl.ds(48, 16)), (0, pl.ds(48, 16)), tile(0, 1), down & east, down & west),
        SE=((1, pl.ds(48, 16)), (5, pl.ds(48, 16)), tile(0, -1), down & west, down & east),
    )
    names = tuple(halo)

    def h_copy(name):
        src, dst, to, _, _ = halo[name]
        j = names.index(name)
        return rc(T.at[src], T.at[dst], hs.at[j], hr.at[j], to)

    def h_start(*which):
        for name in which:
            @pl.when(halo[name][3])
            def _():
                h_copy(name).start()

    def h_wait_send(*which):
        for name in which:
            @pl.when(halo[name][3])
            def _():
                h_copy(name).wait_send()

    def h_wait(*which):
        for name in which:
            d = T.at[halo[name][1]]
            j = names.index(name)

            @pl.when(halo[name][4])
            def _():
                rc(d, d, hs.at[j], hr.at[j], sib).wait_recv()

    a_starts = [a_first(s, i, to) for i in range(3) for s, to in (("X1", xp), ("X2", xm))]
    for c in a_starts:
        c.start()
    sa_send.start()

    def swap_fours(a, b):
        low = lax.broadcasted_iota(jnp.int32, a.shape, 0) < 4
        return jnp.where(low, a, pltpu.roll(b, 4, 0)), jnp.where(low, pltpu.roll(a, 4, 0), b)

    def regroup():
        def step(i, _):
            lanes = pl.ds(pl.multiple_of(i * 256, 256), 256)
            for jj in range(2):
                v = NAT[pl.ds(64 * jj, 64), lanes].astype(jnp.float32)
                for half in range(2):
                    pairs = [swap_fours(v[32 * j + 8 * half : 32 * j + 8 * half + 8], v[32 * j + 16 + 8 * half : 32 * j + 24 + 8 * half]) for j in range(2)]
                    for e in range(2):
                        t = jnp.concatenate([pairs[0][e], pairs[1][e]], axis=0)
                        T[1 + 2 * half + e, 16 + 16 * jj : 32 + 16 * jj, lanes] = t.astype(jnp.bfloat16)
            return 0

        lax.fori_loop(0, 24, step, 0)

    def norm_rows(g, r, own_row=None):
        v = T[g, pl.ds(r, 16), :].astype(jnp.float32)
        mean = jnp.sum(v, axis=1, keepdims=True) * (1.0 / 6144)
        d = v - mean
        var = jnp.sum(d * d, axis=1, keepdims=True) * (1.0 / 6144)
        n = (d * lax.rsqrt(var + 1e-06) * gain[...]).astype(jnp.bfloat16)
        at = pl.multiple_of(g * 64 + r, 16)
        for j in range(GROUPS):
            N[j, pl.ds(at, 16), :] = n[:, j * HD : (j + 1) * HD]
            if own_row is not None:
                NO[j, pl.ds(own_row, 16), :] = n[:, j * HD : (j + 1) * HD]

    def norm_own():
        def step(i, _):
            g, half = i // 2, i % 2
            norm_rows(1 + g, pl.multiple_of(16 + 16 * half, 16), pl.multiple_of(16 * i, 16))
            return 0

        lax.fori_loop(0, 8, step, 0)

    def norm_vertical():
        def step(i, _):
            norm_rows(1 + i // 2, pl.multiple_of(48 * (i % 2), 16))
            return 0

        lax.fori_loop(0, 8, step, 0)

    def norm_sides():
        def step(i, _):
            norm_rows(5 * (i // 4), pl.multiple_of(16 * (i % 4), 16))
            return 0

        lax.fori_loop(0, 8, step, 0)

    def rows_of(ref, cb, part):
        cols = []
        for j in range(KEEP):
            i = qi[cb, j]
            if part == "sides":
                cols.append(jnp.concatenate([ref[i, 0:64, :], ref[i, 320:384, :]], axis=0))
            elif part in ("middle", "both"):
                cols.append(ref[i, 64:320, :])
            else:
                cols.append(ref[i])
        return jnp.concatenate(cols, axis=1)

    def project(ref, cb, part):
        w = W[pl.ds(cb * KEEP, KEEP)].reshape(KEEP * HD, HD)
        return jnp.dot(rows_of(ref, cb, part), w, preferred_element_type=jnp.float32).astype(jnp.bfloat16)

    def chunk(c, part):
        lo = c * 3

        @pl.when(c < HEADS // 3)
        def _():
            if part in ("own", "both", "all"):
                for e in range(3):
                    Q[lo + e] = project(NO, lo + e, "own")

        @pl.when(c >= HEADS // 3)
        def _():
            if part == "own":
                return
            for e in range(3):
                r = project(N, lo + e, part)
                if part in ("middle", "both"):
                    KV[lo + e - HEADS, 64:320, :] = r
                elif part == "sides":
                    KV[lo + e - HEADS, 0:64, :] = r[0:64]
                    KV[lo + e - HEADS, 320:384, :] = r[64:128]
                else:
                    KV[lo + e - HEADS] = r

    def shard(f, part, first=0, last=6):
        def step(c, _):
            chunk(f * 6 + c, part)
            return 0

        lax.fori_loop(first, last, step, 0)

    def make_bias():
        lane = lax.broadcasted_iota(jnp.int32, (8, PAIR), 1)
        sub = lax.broadcasted_iota(jnp.int32, (8, PAIR), 0)
        ky, kx = (lane % 64) // 4 - 4, (lane // 64) * 4 + lane % 4 - 4
        inside = (ky + row * TH >= 0) & (ky + row * TH < 8 * TH)
        low = lax.broadcasted_iota(jnp.int32, (8, HD), 1) < 64
        right = lax.broadcasted_iota(jnp.int32, (8, HD), 1) % 4 >= lax.broadcasted_iota(jnp.int32, (8, HD), 0) % 4
        for i in range(4):
            qy, qx = 2 * i + sub // 4, sub % 4
            ok = inside & (jnp.abs(ky - qy) <= RADIUS) & (jnp.abs(kx - qx) <= RADIUS)

            def step(h, _):
                b = jnp.broadcast_to(base[pl.ds(h, 1), :], (8, 512))
                r = [pltpu.roll(b[:, 128 * e : 128 * e + 128], 8 * i, 1, stride=1, stride_axis=0) for e in range(4)]
                same = jnp.where(right, r[2], r[1])
                first = jnp.where(ok[:, :HD], jnp.where(low, r[0], pltpu.roll(same, 64, 1)), NEG)
                last = jnp.where(ok[:, HD:], r[3], NEG)
                turned = pltpu.roll(first, 64, 1)
                B[h, 8 * i : 8 * i + 8, :] = jnp.concatenate([first, jnp.where(low, last, NEG)], axis=1)
                B[h, 32 + 8 * i : 40 + 8 * i, :] = jnp.concatenate([jnp.where(low, NEG, turned), jnp.where(low, turned, pltpu.roll(last, 64, 1))], axis=1)
                return 0

            lax.fori_loop(0, HEADS, step, 0, unroll=4)
        wide = lax.broadcasted_iota(jnp.int32, (8, PAIR), 1)
        EDGE[0] = jnp.where((wide < 64) & (col == 0), NEG, 0.0)
        EDGE[1] = jnp.where((wide >= 192) & (col == 7), NEG, 0.0)

    def attend(h):
        kk, vv, qq, bias = KV[h], KV[HEADS + h], Q[h], B[h]
        outs = []
        for p in range(2):
            s = lax.dot_general(
                qq[64 * p : 64 * p + 64], kk[128 * p : 128 * p + PAIR], (((1,), (1,)), ((), ())), preferred_element_type=jnp.float32
            )
            s = s * (HD ** -0.5) + bias + EDGE[p, 0:1, :]
            m = jnp.max(s, axis=1, keepdims=True)
            w = jnp.exp(s - m)
            total = jnp.sum(w, axis=1, keepdims=True)
            o = jnp.dot(w.astype(jnp.bfloat16), vv[128 * p : 128 * p + PAIR], preferred_element_type=jnp.float32) / total
            outs += [o[0:32], o[32:64]]
        for j in range(4):
            halves = []
            for half in range(2):
                halves.append(swap_fours(outs[2 * half][8 * j : 8 * j + 8], outs[2 * half + 1][8 * j : 8 * j + 8]))
            for e in range(2):
                ATT[h, 32 * j + 16 * e : 32 * j + 16 * e + 16, :] = jnp.concatenate([halves[0][e], halves[1][e]], axis=0).astype(jnp.bfloat16)

    def output(cb):
        lhs = jnp.concatenate([ATT[oi[cb, j]] for j in range(KEEP_O)], axis=1)
        w = WO[pl.ds(cb * KEEP_O, KEEP_O)].reshape(KEEP_O * HD, HD)
        acc = jnp.dot(lhs, w, preferred_element_type=jnp.float32)
        lanes = pl.ds(pl.multiple_of(cb * HD, HD), HD)
        out[:, lanes] = (acc + NAT[:, lanes].astype(jnp.float32)).astype(jnp.bfloat16)

    c_tok.wait()
    regroup()
    h_start("N", "S", "W", "E")

    @pl.when(jnp.logical_not(up))
    def _():
        T[:, 0:16, :] = jnp.zeros((6, 16, 6144), jnp.bfloat16)

    @pl.when(jnp.logical_not(down))
    def _():
        T[:, 48:64, :] = jnp.zeros((6, 16, 6144), jnp.bfloat16)

    @pl.when(jnp.logical_not(west))
    def _():
        T[0] = jnp.zeros((64, 6144), jnp.bfloat16)

    @pl.when(jnp.logical_not(east))
    def _():
        T[5] = jnp.zeros((64, 6144), jnp.bfloat16)

    def pump_x(sub):
        for s in ("X1", "X2"):
            a_recv(s, sub).wait_recv()
        a_forward("X2", "Z1", sub, zp).start()
        a_forward("X2", "Y2", sub, ym).start()
        a_forward("X1", "Y1", sub, yp).start()
        s_send("X1", sub).start()
        s_send("X2", sub).start()

    def pump_yz(sub):
        for s in ("Y2", "Y1", "Z1"):
            a_recv(s, sub).wait_recv()
            if s == "Y2":
                a_forward("Y2", "Z2", sub, zm).start()
            s_send(s, sub).start()

    norm_own()
    pump_x(0)
    make_bias()
    pump_x(1)
    c_wq.wait()
    shard(f_own, "own")
    sa_recv.wait_recv()
    shard(f_sib, "own")
    pump_x(2)
    o_starts = [o_first("X1", xp), o_first("X2", xm)]
    for c in o_starts:
        c.start()
    sb_send.start()

    h_wait("N", "S")
    h_start("NW", "NE", "SW", "SE")
    norm_vertical()
    pump_yz(0)
    shard(f_own, "middle")
    pump_yz(1)
    shard(f_sib, "middle")
    pump_yz(2)

    def received(s, part):
        chunk(f_oth * 6 + chunk_of[s], part)
        for i in range(3):
            s_recv(s, i).wait_recv()
        chunk(f_osb * 6 + chunk_of[s], part)

    def again(s):
        chunk(f_oth * 6 + chunk_of[s], "sides")
        chunk(f_osb * 6 + chunk_of[s], "sides")

    for s in ("X1", "X2"):
        received(s, "both")
    for s in ("X1", "X2"):
        o_recv(s).wait_recv()
        os_send(s).start()
    o_forward("X2", "Z1", zp).start()
    o_forward("X2", "Y2", ym).start()
    o_forward("X1", "Y1", yp).start()
    h_wait("W", "E", "NW", "NE", "SW", "SE")
    norm_sides()
    for i in range(3):
        a_recv("Z2", i).wait_recv()
        s_send("Z2", i).start()
    for s in ("Y2", "Y1", "Z1"):
        o_recv(s).wait_recv()
        os_send(s).start()
        if s == "Y2":
            o_forward("Y2", "Z2", zm).start()
    shard(f_own, "sides")
    shard(f_sib, "sides")
    for s in ("X1", "X2"):
        again(s)
    for s in ("Y1", "Y2", "Z1", "Z2"):
        received(s, "all")

    def head(h, _):
        attend(h)
        return 0

    lax.fori_loop(0, HEADS, head, 0, unroll=2)

    o_recv("Z2").wait_recv()
    os_send("Z2").start()
    c_wo.wait()
    sb_recv.wait_recv()
    for s in STAGES:
        os_recv(s).wait_recv()

    def column(cb, _):
        output(cb)
        return 0

    lax.fori_loop(0, GROUPS, column, 0, unroll=4)

    for c in a_starts + o_starts + [sa_send, sb_send]:
        c.wait_send()
    for have, s, to in (("X2", "Z1", zp), ("X2", "Y2", ym), ("X1", "Y1", yp), ("Y2", "Z2", zm)):
        for i in range(3):
            a_forward(have, s, i, to).wait_send()
        o_forward(have, s, to).wait_send()
    for s in STAGES:
        for i in range(3):
            s_send(s, i).wait_send()
        os_send(s).wait_send()
    h_wait_send(*names)


def body(tokens, ln_gain, qkv_blocks, qkv_index, out_blocks, out_index, rel_bias):
    square = rel_bias.reshape(HEADS, 9, 9)
    wide = lambda cols: jnp.pad(square[:, :, cols : cols + 4].reshape(HEADS, 36), ((0, 0), (0, HD - 36)))
    base = jnp.concatenate([wide(0), jnp.roll(wide(0), -4, axis=1), wide(4), jnp.roll(wide(5), -3, axis=1)], axis=1)
    any_, vmem, smem = pl.BlockSpec(memory_space=pl.ANY), pl.BlockSpec(memory_space=pltpu.VMEM), pl.BlockSpec(memory_space=pltpu.SMEM)
    dma = lambda n: pltpu.SemaphoreType.DMA((n,))
    bf = jnp.bfloat16
    mixed = pl.pallas_call(
        kernel,
        out_shape=jax.ShapeDtypeStruct((OWN, 6144), bf),
        in_specs=[smem, smem, any_, vmem, vmem, any_, any_],
        out_specs=vmem,
        scratch_shapes=[
            pltpu.VMEM((OWN, 6144), bf),
            pltpu.VMEM((6, 64, 6144), bf),
            pltpu.VMEM((GROUPS, ALL, HD), bf),
            pltpu.VMEM((GROUPS, OWN, HD), bf),
            pltpu.VMEM((432, HD, HD), bf),
            pltpu.VMEM((144, HD, HD), bf),
            pltpu.VMEM((HEADS, OWN, HD), bf),
            pltpu.VMEM((2 * HEADS, ALL, HD), bf),
            pltpu.VMEM((HEADS, OWN, HD), bf),
            pltpu.VMEM((HEADS, 64, PAIR), jnp.float32),
            pltpu.VMEM((2, 8, PAIR), jnp.float32),
            dma(3), dma(8), dma(8), dma(18), dma(18), dma(18), dma(18), dma(6), dma(6), dma(6), dma(6), dma(2), dma(2),
        ],
        compiler_params=pltpu.CompilerParams(collective_id=0, has_side_effects=True, vmem_limit_bytes=58 * 2**20),
        cost_estimate=pl.CostEstimate(flops=6 * 10**9, bytes_accessed=30 * 2**20, transcendentals=10**6),
        name="block",
    )(
        qkv_index, out_index, tokens.reshape(OWN, -1), ln_gain.reshape(1, -1), base,
        qkv_blocks.reshape(SHARD * KEEP, HD, HD), out_blocks.reshape(SHARD_O * KEEP_O, HD, HD),
    )
    return mixed.reshape(1, TH, TW, -1)


def solution(mesh):
    in_specs = (
        P("fsdp", "row", "col", None),
        P(),
        P("fsdp", None, None, None),
        P(),
        P("fsdp", None, None, None),
        P(),
        P(),
    )
    out_specs = P("fsdp", "row", "col", None)
    return jax.shard_map(body, mesh=mesh, in_specs=in_specs, out_specs=out_specs, check_vma=False)
```

time: 362 us -> 98.1 us (0.27); the launches traced: 358 us -> 97.8 us
  waiting for transfers between devices: 153 us -> 0 us
  Pallas kernels: 0 us -> 90.3 us
  local copies, waits for them, and re-layouts: 86 us -> 7.39 us
  matrix products: 42.6 us -> 0 us
  loops' own time: 30.8 us -> 0 us
  other arithmetic: 16.5 us -> 0 us
  starting transfers between devices: 15.7 us -> 0 us
  between operations: 13.6 us -> 0.04 us
    all_gather x2 -> x0, waiting for transfers between devices: 115 us -> none  [the longest x1 115 us: body(): lax.all_gather(qkv_blocks, 'fsdp', axis=0, tiled=True)]
    pallas_call x0 -> x1, Pallas kernels: none -> 90.3 us  [body(): pl.pallas_call(kernel, out_shape=jax.ShapeDtypeStruct((OWN, 6144), bf), i...]
    dot_general x19 -> x0, matrix products: 42.6 us -> none  [the longest x8 17.8 us: one_row(): jnp.einsum('xhd,rchd->hxrc', query_heads[row_at], key_slab, preferred_ele...]
    ppermute x4 -> x0, waiting for transfers between devices: 36.8 us -> none  [the longest x2 24.8 us: with_halo(): before = lax.ppermute(last, axis, up)]
    another operation x1 -> x0, loops' own time: 30.8 us -> none  [neighbourhood(): return lax.map(one_row, jnp.arange(tile_rows, dtype=jnp.int32))]
    while x24 -> x0, local copies, waits for them, and re-layouts: 23.7 us -> none
    gather x2 -> x0, local copies, waits for them, and re-layouts: 21.1 us -> none  [block_product(): picked = jnp.take(blocks_of, block_ids, axis=1)]
    ppermute x4 -> x0, starting transfers between devices: 15.7 us -> none  [the longest x2 8 us: with_halo(): after = lax.ppermute(leading, axis, down)]
  transfers between devices with their start and end apart: 6 -> 0, of which waited for: 5 -> 0; matrix products, arithmetic and copies ran while one was open for 31% -> 0% of each run, Pallas kernels for 0% -> 0%
where the time goes in v2:
time: 98.1 us; the launch traced here: 97.8 us
  Pallas kernels  90.3 us (92%)
  local copies, waits for them, and re-layouts  7.39 us (8%)
    pallas_call x1, Pallas kernels, body(): pl.pallas_call(kernel, out_shape=jax.ShapeDtypeStruct((OWN, 6144), bf), i...  90.3 us
    unnamed x4, local copies, waits for them, and re-layouts  6.25 us

profile of v2, /device:TPU:101, one launch (start us, length us, event | category | flops | bytes accessed | tf_op | source)
XLA Modules:
  0.0 97.8 jit_solution(2002097759961362632)
XLA Ops:
  0.0 1.4 %copy.17.oi = s32[48,3]{1,0:T(8,128)} copy(s32[48,3]{0,1:T(4,128)} %param.12) | data formatting | bytes 1152 | tf_op args[5]
  1.4 1.4 %copy.16.qi = s32[72,6]{1,0:T(8,128)} copy(s32[72,6]{0,1:T(8,128)} %param.10) | data formatting | bytes 3456 | tf_op args[3]
  2.8 0.8 copy.10
  3.6 0.1 copy.14
  3.7 0.1 pad_slice_fusion
  3.8 0.1 copy.13
  3.9 0.1 copy.11
  4.0 0.1 pad_slice_fusion.1
  4.0 0.7 concatenate.8.base
  4.7 90.3 %block.1 = bf16[128,6144]{1,0:T(8,128)(2,1)} custom-call(s32[72,6]{1,0:T(8,128)} %copy.16.qi, s32[48,3]{1,0:T(8,128)} %copy.17.oi, bf16[128,6144]{1,0:T(8,128)(2,1)} %bitcast.19, f32[1,6144]{1,0:T(1,128)} %bitcast.21, f32[24,512]{1,0:T(8,128)} %concatenate.8.base, bf16[108,128,128]{2,1,0:T(8,128)(2,1)} %bitcast.18, bf16[36,128,128]{2,1,0:T(8,128)(2,1)} %bitcast.20), custom_call_target="tpu_custom_call" | custom-call | flops 6000000000 | bytes 31457280 | tf_op jit(solution)/shard_map/block/pallas_call | solution.py:461
  95.1 2.7 %copy.19 = bf16[1,8,16,6144]{3,2,1,0:T(8,128)(2,1)} copy(bf16[1,8,16,6144]{3,2,1,0:T(8,128)(2,1)} %bitcast.15) | data formatting | bytes 3145728
  (7 shorter events, 0.1 us)

commit v3 on v2

v3 whole, which is shorter than its diff:
```python
import jax
import jax.numpy as jnp
from jax import lax
from jax.experimental import pallas as pl
from jax.experimental.pallas import tpu as pltpu
from jax.sharding import PartitionSpec as P

MESH = pl.DeviceIdType.MESH
HD = 128
HEADS = 24
KEEP = 6
KEEP_O = 3
RADIUS = 4
TH, TW = 8, 16
OWN = TH * TW
ALL = (TH + 2 * RADIUS) * (TW + 2 * RADIUS)
PAIR = 256
GROUPS = 48
SHARD = 18
SHARD_O = 12
NEG = -1e30


def kernel(
    qi_any, oi_any, tok, gain, rel, wq, wo, out,
    NAT, T, N, NO, W, WO, Q, KV, ATT, B, EDGE, SHIFT, QI, OI,
    loc, hs, hr, ws, wr, ss, sr, bs, br, bss, bsr, os, orr,
):
    row, col, fs_ = lax.axis_index("row"), lax.axis_index("col"), lax.axis_index("fsdp")
    x, y, z, k = (row // 4) * 2 + fs_ // 2, row % 4, col, fs_ % 2

    def dev(dx, dy, dz, dk):
        xx, yy, zz, kk = (x + dx) % 4, (y + dy) % 4, (z + dz) % 8, (k + dk) % 2
        return ((xx // 2) * 4 + yy, zz, (xx % 2) * 2 + kk)

    def tile(dr, dc):
        return ((row + dr + 8) % 8, (col + dc + 8) % 8, fs_)

    f_own = fs_
    f_sib = (x % 2) * 2 + (1 - k)
    f_oth = (1 - x % 2) * 2 + k
    f_osb = (1 - x % 2) * 2 + (1 - k)
    cz, cy = z % 2, y % 2
    sib = dev(0, 0, 0, 1)
    xp, xm = dev(1, 0, 0, 0), dev(3, 0, 0, 0)
    yp, ym = dev(0, 1, 0, 0), dev(0, 3, 0, 0)
    zp, zm = dev(0, 0, 1, 0), dev(0, 0, 7, 0)
    ya, yb, za, zb = 4 * cy, 4 * (1 - cy), 8 + 4 * cz, 8 + 4 * (1 - cz)
    came = [ya + i for i in range(4)] + [za + i for i in range(4)] + [16, 17] + [yb + i for i in range(4)] + [zb + i for i in range(4)]

    c_qi = pltpu.make_async_copy(qi_any, QI, loc.at[3])
    c_oi = pltpu.make_async_copy(oi_any, OI, loc.at[4])
    c_qi.start()
    c_oi.start()
    c_tok = pltpu.make_async_copy(tok, NAT, loc.at[0])
    c_wq = pltpu.make_async_copy(wq, W.at[pl.ds(f_own * 108, 108)], loc.at[1])
    c_wo = pltpu.make_async_copy(wo, WO.at[pl.ds(f_own * 36, 36)], loc.at[2])
    c_tok.start()
    c_wq.start()
    c_wo.start()

    partners = [sib, xp, xm, yp, ym, zp, zm, tile(1, 0), tile(-1, 0), dev(2, 0, 0, 0)]
    barrier = pltpu.get_barrier_semaphore()
    for p in partners:
        pl.semaphore_signal(barrier, inc=1, device_id=p, device_id_type=MESH)
    pl.semaphore_wait(barrier, len(partners))

    def rc(src, dst, s, r, to):
        return pltpu.make_async_remote_copy(src_ref=src, dst_ref=dst, send_sem=s, recv_sem=r, device_id=to, device_id_type=MESH)

    def a_ref(f, j):
        return W.at[pl.ds((f * SHARD + came[j]) * KEEP, KEEP)]

    def a_first(j):
        src = wq.at[pl.ds(came[j] * KEEP, KEEP)]
        return rc(src, a_ref(f_own, j), ws.at[j], wr.at[j], xp if j < 4 or j == 8 else xm)

    def a_forward(j):
        d = a_ref(f_oth, j)
        to = (yp, ym, zp, zm)[(j // 4) * 2 + j % 2]
        return rc(d, d, ws.at[10 + j], wr.at[10 + j], to)

    def a_recv(j):
        d = a_ref(f_oth, j)
        return rc(d, d, ws.at[j], wr.at[j], sib)

    def s_send(j):
        d = a_ref(f_oth, j)
        return rc(d, d, ss.at[j], sr.at[j], sib)

    def s_recv(j):
        d = a_ref(f_osb, j)
        return rc(d, d, ss.at[j], sr.at[j], sib)

    parts = [cy, 2 + cz, 1 - cy, 2 + 1 - cz]

    def o_ref(f, j):
        return WO.at[pl.ds(f * 36 + parts[j] * 9, 9)]

    def o_first(j):
        return rc(wo.at[pl.ds(parts[j] * 9, 9)], o_ref(f_own, j), bs.at[j], br.at[j], (xp, xm)[j])

    def o_forward(j):
        d = o_ref(f_oth, j)
        return rc(d, d, bs.at[2 + j], br.at[2 + j], (yp, zp)[j])

    def o_recv(j):
        d = o_ref(f_oth, j)
        return rc(d, d, bs.at[j], br.at[j], sib)

    def os_send(j):
        d = o_ref(f_oth, j)
        return rc(d, d, bss.at[j], bsr.at[j], sib)

    def os_recv(j):
        d = o_ref(f_osb, j)
        return rc(d, d, bss.at[j], bsr.at[j], sib)

    sa_send = rc(wq, W.at[pl.ds(f_own * 108, 108)], os.at[0], orr.at[0], sib)
    d_sa = W.at[pl.ds(f_sib * 108, 108)]
    sa_recv = rc(d_sa, d_sa, os.at[0], orr.at[0], sib)
    sb_send = rc(wo, WO.at[pl.ds(f_own * 36, 36)], os.at[1], orr.at[1], sib)
    d_sb = WO.at[pl.ds(f_sib * 36, 36)]
    sb_recv = rc(d_sb, d_sb, os.at[1], orr.at[1], sib)

    up, down, west, east = row > 0, row < 7, col > 0, col < 7
    four, low2, high2, across = pl.ds(1, 4), pl.ds(1, 2), pl.ds(3, 2), dev(2, 0, 0, 0)
    halo = dict(
        N=((four, pl.ds(32, 16)), (four, pl.ds(0, 16)), tile(1, 0), down & (row != 3), up & (row != 4)),
        S=((four, pl.ds(16, 16)), (four, pl.ds(48, 16)), tile(-1, 0), up & (row != 4), down & (row != 3)),
        W=((4, pl.ds(16, 32)), (0, pl.ds(16, 32)), tile(0, 1), east, west),
        E=((1, pl.ds(16, 32)), (5, pl.ds(16, 32)), tile(0, -1), west, east),
        NW=((4, pl.ds(0, 16)), (0, pl.ds(0, 16)), tile(0, 1), up & east, up & west),
        NE=((1, pl.ds(0, 16)), (5, pl.ds(0, 16)), tile(0, -1), up & west, up & east),
        SW=((4, pl.ds(48, 16)), (0, pl.ds(48, 16)), tile(0, 1), down & east, down & west),
        SE=((1, pl.ds(48, 16)), (5, pl.ds(48, 16)), tile(0, -1), down & west, down & east),
        ND=((low2, pl.ds(32, 16)), (low2, pl.ds(0, 16)), tile(1, 0), row == 3, row == 4),
        NR=((high2, pl.ds(32, 16)), (high2, pl.ds(0, 16)), yp, row == 3, row == 0),
        NF=((high2, pl.ds(0, 16)), (high2, pl.ds(0, 16)), across, row == 0, row == 4),
        SD=((low2, pl.ds(16, 16)), (low2, pl.ds(48, 16)), tile(-1, 0), row == 4, row == 3),
        SR=((high2, pl.ds(16, 16)), (high2, pl.ds(48, 16)), ym, row == 4, row == 7),
        SF=((high2, pl.ds(48, 16)), (high2, pl.ds(48, 16)), across, row == 7, row == 3),
    )
    names = tuple(halo)

    def h_copy(name):
        src, dst, to, _, _ = halo[name]
        j = names.index(name)
        return rc(T.at[src], T.at[dst], hs.at[j], hr.at[j], to)

    def h_start(*which):
        for name in which:
            @pl.when(halo[name][3])
            def _():
                h_copy(name).start()

    def h_wait_send(*which):
        for name in which:
            @pl.when(halo[name][3])
            def _():
                h_copy(name).wait_send()

    def h_wait(*which):
        for name in which:
            d = T.at[halo[name][1]]
            j = names.index(name)

            @pl.when(halo[name][4])
            def _():
                rc(d, d, hs.at[j], hr.at[j], sib).wait_recv()

    a_starts = [a_first(j) for j in (0, 4, 1, 5, 2, 6, 3, 7, 8, 9)]
    for c in a_starts:
        c.start()
    sa_send.start()

    def swap_fours(a, b):
        low = lax.broadcasted_iota(jnp.int32, a.shape, 0) < 4
        return jnp.where(low, a, pltpu.roll(b, 4, 0)), jnp.where(low, pltpu.roll(a, 4, 0), b)

    def regroup():
        def step(i, _):
            lanes = pl.ds(pl.multiple_of(i * 256, 256), 256)
            for jj in range(2):
                v = NAT[pl.ds(64 * jj, 64), lanes].astype(jnp.float32)
                for half in range(2):
                    pairs = [swap_fours(v[32 * j + 8 * half : 32 * j + 8 * half + 8], v[32 * j + 16 + 8 * half : 32 * j + 24 + 8 * half]) for j in range(2)]
                    for e in range(2):
                        t = jnp.concatenate([pairs[0][e], pairs[1][e]], axis=0)
                        T[1 + 2 * half + e, 16 + 16 * jj : 32 + 16 * jj, lanes] = t.astype(jnp.bfloat16)
            return 0

        lax.fori_loop(0, 24, step, 0)

    def norm_rows(g, r, own_row=None):
        v = T[g, pl.ds(r, 16), :].astype(jnp.float32)
        mean = jnp.sum(v, axis=1, keepdims=True) * (1.0 / 6144)
        d = v - mean
        var = jnp.sum(d * d, axis=1, keepdims=True) * (1.0 / 6144)
        n = (d * lax.rsqrt(var + 1e-06) * gain[...]).astype(jnp.bfloat16)
        at = pl.multiple_of(g * 64 + r, 16)
        for j in range(GROUPS):
            N[j, pl.ds(at, 16), :] = n[:, j * HD : (j + 1) * HD]
            if own_row is not None:
                NO[j, pl.ds(own_row, 16), :] = n[:, j * HD : (j + 1) * HD]

    def norm_own():
        def step(i, _):
            g, half = i // 2, i % 2
            norm_rows(1 + g, pl.multiple_of(16 + 16 * half, 16), pl.multiple_of(16 * i, 16))
            return 0

        lax.fori_loop(0, 8, step, 0)

    def norm_vertical():
        def step(i, _):
            norm_rows(1 + i // 2, pl.multiple_of(48 * (i % 2), 16))
            return 0

        lax.fori_loop(0, 8, step, 0)

    def norm_sides():
        def step(i, _):
            norm_rows(5 * (i // 4), pl.multiple_of(16 * (i % 4), 16))
            return 0

        lax.fori_loop(0, 8, step, 0)

    def rows_of(ref, cb, part):
        cols = []
        for j in range(KEEP):
            i = QI[j, cb]
            if part == "sides":
                cols.append(jnp.concatenate([ref[i, 0:64, :], ref[i, 320:384, :]], axis=0))
            elif part in ("middle", "both"):
                cols.append(ref[i, 64:320, :])
            else:
                cols.append(ref[i])
        return jnp.concatenate(cols, axis=1)

    def project(ref, cb, part):
        w = W[pl.ds(cb * KEEP, KEEP)].reshape(KEEP * HD, HD)
        return jnp.dot(rows_of(ref, cb, part), w, preferred_element_type=jnp.float32).astype(jnp.bfloat16)

    def chunk(lo, count, part):
        @pl.when(lo < HEADS)
        def _():
            if part in ("own", "both", "all"):
                for e in range(count):
                    Q[lo + e] = project(NO, lo + e, "own")

        @pl.when(lo >= HEADS)
        def _():
            if part == "own":
                return
            for e in range(count):
                r = project(N, lo + e, part)
                if part in ("middle", "both"):
                    KV[lo + e - HEADS, 64:320, :] = r
                elif part == "sides":
                    KV[lo + e - HEADS, 0:64, :] = r[0:64]
                    KV[lo + e - HEADS, 320:384, :] = r[64:128]
                else:
                    KV[lo + e - HEADS] = r

    def shard(f, part):
        def step(c, _):
            chunk(f * SHARD + c * 3, 3, part)
            return 0

        lax.fori_loop(0, SHARD // 3, step, 0)

    def make_shifted():
        SHIFT[0] = jnp.zeros((HEADS, HD), jnp.float32)
        SHIFT[0, :, 0:81] = rel[...]
        v = SHIFT[0]
        lane = lax.broadcasted_iota(jnp.int32, (HEADS, HD), 1)
        rows = [jnp.zeros_like(v)] * 3
        for a in range(9):
            for e in range(3):
                at = (lane + (3 if e == 2 else 0)) % HD
                moved = pltpu.roll(v, (-5 * a - 4 * e) % HD, 1)
                rows[e] = jnp.where((at >= 4 * a) & (at < 4 * a + 4), moved, rows[e])
        SHIFT[0] = rows[0]
        SHIFT[1] = pltpu.roll(rows[0], HD - 4, 1)
        SHIFT[2] = rows[1]
        SHIFT[3] = rows[2]

    def make_bias():
        make_shifted()
        lane = lax.broadcasted_iota(jnp.int32, (8, PAIR), 1)
        sub = lax.broadcasted_iota(jnp.int32, (8, PAIR), 0)
        ky, kx = (lane % 64) // 4 - 4, (lane // 64) * 4 + lane % 4 - 4
        inside = (ky + row * TH >= 0) & (ky + row * TH < 8 * TH)
        low = lax.broadcasted_iota(jnp.int32, (8, HD), 1) < 64
        right = lax.broadcasted_iota(jnp.int32, (8, HD), 1) % 4 >= lax.broadcasted_iota(jnp.int32, (8, HD), 0) % 4
        for i in range(4):
            qy, qx = 2 * i + sub // 4, sub % 4
            ok = inside & (jnp.abs(ky - qy) <= RADIUS) & (jnp.abs(kx - qx) <= RADIUS)

            def step(h, _):
                r = [
                    pltpu.roll(jnp.broadcast_to(SHIFT[e, pl.ds(h, 1), :], (8, HD)), 8 * i, 1, stride=1, stride_axis=0) for e in range(4)
                ]
                same = jnp.where(right, r[2], r[1])
                first = jnp.where(ok[:, :HD], jnp.where(low, r[0], pltpu.roll(same, 64, 1)), NEG)
                last = jnp.where(ok[:, HD:], r[3], NEG)
                turned = pltpu.roll(first, 64, 1)
                B[h, 8 * i : 8 * i + 8, :] = jnp.concatenate([first, jnp.where(low, last, NEG)], axis=1)
                B[h, 32 + 8 * i : 40 + 8 * i, :] = jnp.concatenate([jnp.where(low, NEG, turned), jnp.where(low, turned, pltpu.roll(last, 64, 1))], axis=1)
                return 0

            lax.fori_loop(0, HEADS, step, 0, unroll=4)
        wide = lax.broadcasted_iota(jnp.int32, (8, PAIR), 1)
        EDGE[0] = jnp.where((wide < 64) & (col == 0), NEG, 0.0)
        EDGE[1] = jnp.where((wide >= 192) & (col == 7), NEG, 0.0)

    def attend(h0, count):
        pairs = [(h0 + i, p) for i in range(count) for p in range(2)]
        ss_, ws_, os_ = [], [], []
        for h, p in pairs:
            ss_.append(lax.dot_general(
                Q[h, 64 * p : 64 * p + 64, :], KV[h, 128 * p : 128 * p + PAIR, :], (((1,), (1,)), ((), ())), preferred_element_type=jnp.float32
            ))
        for (h, p), s in zip(pairs, ss_):
            s = s * (HD ** -0.5) + B[h] + EDGE[p, 0:1, :]
            w = jnp.exp(s - jnp.max(s, axis=1, keepdims=True))
            ws_.append((w.astype(jnp.bfloat16), jnp.sum(w, axis=1, keepdims=True)))
        for (h, p), (w, total) in zip(pairs, ws_):
            o = jnp.dot(w, KV[HEADS + h, 128 * p : 128 * p + PAIR, :], preferred_element_type=jnp.float32) / total
            os_.append((o[0:32], o[32:64]))
        for i in range(count):
            outs = os_[2 * i] + os_[2 * i + 1]
            for j in range(4):
                halves = []
                for half in range(2):
                    halves.append(swap_fours(outs[2 * half][8 * j : 8 * j + 8], outs[2 * half + 1][8 * j : 8 * j + 8]))
                for e in range(2):
                    both = jnp.concatenate([halves[0][e], halves[1][e]], axis=0)
                    ATT[h0 + i, 32 * j + 16 * e : 32 * j + 16 * e + 16, :] = both.astype(jnp.bfloat16)

    def output(cb):
        lhs = jnp.concatenate([ATT[OI[j, cb]] for j in range(KEEP_O)], axis=1)
        w = WO[pl.ds(cb * KEEP_O, KEEP_O)].reshape(KEEP_O * HD, HD)
        acc = jnp.dot(lhs, w, preferred_element_type=jnp.float32)
        lanes = pl.ds(pl.multiple_of(cb * HD, HD), HD)
        out[:, lanes] = (acc + NAT[:, lanes].astype(jnp.float32)).astype(jnp.bfloat16)

    c_tok.wait()
    regroup()
    h_start("NR", "SR", "N", "S", "ND", "SD", "W", "E")

    @pl.when(jnp.logical_not(up))
    def _():
        T[0:3, 0:16, :] = jnp.zeros((3, 16, 6144), jnp.bfloat16)
        T[5, 0:16, :] = jnp.zeros((16, 6144), jnp.bfloat16)

    @pl.when(jnp.logical_not(down))
    def _():
        T[0:3, 48:64, :] = jnp.zeros((3, 16, 6144), jnp.bfloat16)
        T[5, 48:64, :] = jnp.zeros((16, 6144), jnp.bfloat16)

    @pl.when(jnp.logical_not(west))
    def _():
        T[0] = jnp.zeros((64, 6144), jnp.bfloat16)

    @pl.when(jnp.logical_not(east))
    def _():
        T[5] = jnp.zeros((64, 6144), jnp.bfloat16)

    def pump_x(i):
        for j in (i, 4 + i):
            a_recv(j).wait_recv()
            a_forward(j).start()
            s_send(j).start()

    def pump(*items):
        for j in items:
            a_recv(j).wait_recv()
            s_send(j).start()

    norm_own()
    pump_x(0)
    make_bias()
    pump_x(1)
    c_wq.wait()
    c_qi.wait()
    shard(f_own, "own")
    pump_x(2)
    h_wait("NR", "SR")
    h_start("NF", "SF")
    o_starts = [o_first(0), o_first(1)]
    for c in o_starts:
        c.start()
    sb_send.start()
    sa_recv.wait_recv()
    shard(f_sib, "own")
    pump_x(3)
    h_wait("N", "S", "ND", "SD", "NF", "SF")
    h_start("NW", "NE", "SW", "SE")
    norm_vertical()
    pump(8, 9, 10, 14)
    for j in range(2):
        o_recv(j).wait_recv()
        o_forward(j).start()
        os_send(j).start()
    shard(f_own, "middle")
    pump(11, 15, 12, 16)
    shard(f_sib, "middle")
    pump(13, 17)

    def received(j, part):
        chunk(f_oth * SHARD + came[j], 2, part)
        for i in range(2):
            s_recv(j + i).wait_recv()
        chunk(f_osb * SHARD + came[j], 2, part)

    for j in (0, 4, 2, 6, 8):
        received(j, "both")
    h_wait("W", "E", "NW", "NE", "SW", "SE")
    norm_sides()
    shard(f_own, "sides")
    shard(f_sib, "sides")
    for j in (0, 4, 2, 6, 8):
        chunk(f_oth * SHARD + came[j], 2, "sides")
        chunk(f_osb * SHARD + came[j], 2, "sides")
    for j in (10, 14, 12, 16):
        received(j, "all")

    def head(i, _):
        attend(3 * i, 3)
        return 0

    lax.fori_loop(0, HEADS // 3, head, 0)

    for j in range(2, 4):
        o_recv(j).wait_recv()
        os_send(j).start()
    c_wo.wait()
    c_oi.wait()
    sb_recv.wait_recv()
    for j in range(4):
        os_recv(j).wait_recv()

    def column(cb, _):
        output(cb)
        return 0

    lax.fori_loop(0, GROUPS, column, 0, unroll=4)

    for c in a_starts + o_starts + [sa_send, sb_send]:
        c.wait_send()
    for j in range(8):
        a_forward(j).wait_send()
    for j in range(2):
        o_forward(j).wait_send()
    for j in range(18):
        s_send(j).wait_send()
    for j in range(4):
        os_send(j).wait_send()
    h_wait_send(*names)


def body(tokens, ln_gain, qkv_blocks, qkv_index, out_blocks, out_index, rel_bias):
    any_, vmem = pl.BlockSpec(memory_space=pl.ANY), pl.BlockSpec(memory_space=pltpu.VMEM)
    dma = lambda n: pltpu.SemaphoreType.DMA((n,))
    bf = jnp.bfloat16
    mixed = pl.pallas_call(
        kernel,
        out_shape=jax.ShapeDtypeStruct((OWN, 6144), bf),
        in_specs=[any_, any_, any_, vmem, vmem, any_, any_],
        out_specs=vmem,
        scratch_shapes=[
            pltpu.VMEM((OWN, 6144), bf),
            pltpu.VMEM((6, 64, 6144), bf),
            pltpu.VMEM((GROUPS, ALL, HD), bf),
            pltpu.VMEM((GROUPS, OWN, HD), bf),
            pltpu.VMEM((432, HD, HD), bf),
            pltpu.VMEM((144, HD, HD), bf),
            pltpu.VMEM((HEADS, OWN, HD), bf),
            pltpu.VMEM((2 * HEADS, ALL, HD), bf),
            pltpu.VMEM((HEADS, OWN, HD), bf),
            pltpu.VMEM((HEADS, 64, PAIR), jnp.float32),
            pltpu.VMEM((2, 8, PAIR), jnp.float32),
            pltpu.VMEM((4, HEADS, HD), jnp.float32),
            pltpu.SMEM((KEEP, 3 * HEADS), jnp.int32),
            pltpu.SMEM((KEEP_O, GROUPS), jnp.int32),
            dma(5), dma(14), dma(14), dma(18), dma(18), dma(18), dma(18), dma(4), dma(4), dma(4), dma(4), dma(2), dma(2),
        ],
        compiler_params=pltpu.CompilerParams(collective_id=0, has_side_effects=True, vmem_limit_bytes=58 * 2**20),
        cost_estimate=pl.CostEstimate(flops=6 * 10**9, bytes_accessed=30 * 2**20, transcendentals=10**6),
        name="block",
    )(
        qkv_index.T, out_index.T, tokens.reshape(OWN, -1), ln_gain.reshape(1, -1), rel_bias,
        qkv_blocks.reshape(SHARD * KEEP, HD, HD), out_blocks.reshape(SHARD_O * KEEP_O, HD, HD),
    )
    return mixed.reshape(1, TH, TW, -1)


def solution(mesh):
    in_specs = (
        P("fsdp", "row", "col", None),
        P(),
        P("fsdp", None, None, None),
        P(),
        P("fsdp", None, None, None),
        P(),
        P(),
    )
    out_specs = P("fsdp", "row", "col", None)
    return jax.shard_map(body, mesh=mesh, in_specs=in_specs, out_specs=out_specs, check_vma=False)
```

time: 98.1 us -> 77.9 us (0.79)
  the two profiles are of different devices: /device:TPU:101 before, /device:TPU:27 now
where the time goes in v3:
time: 77.9 us; the launch traced here: 77.7 us
  Pallas kernels  75 us (96%)
  local copies, waits for them, and re-layouts  2.69 us (3%)
    pallas_call x1, Pallas kernels, body(): pl.pallas_call(kernel, out_shape=jax.ShapeDtypeStruct((OWN, 6144), bf), i...  75 us
    unnamed x1, local copies, waits for them, and re-layouts  2.69 us

profile of v3, /device:TPU:27, one launch (start us, length us, event | category | flops | bytes accessed | tf_op | source)
XLA Modules:
  0.0 77.7 jit_solution(7877863442903473458)
XLA Ops:
  0.0 75.0 %block.1 = bf16[128,6144]{1,0:T(8,128)(2,1)} custom-call(s32[6,72]{1,0:T(8,128)} %bitcast.12, s32[3,48]{1,0:T(4,128)} %bitcast.13, bf16[128,6144]{1,0:T(8,128)(2,1)} %bitcast.9, f32[1,6144]{1,0:T(1,128)} %bitcast.11, f32[24,81]{1,0:T(8,128)} %rel.1, bf16[108,128,128]{2,1,0:T(8,128)(2,1)} %bitcast.8, bf16[36,128,128]{2,1,0:T(8,128)(2,1)} %bitcast.10), custom_call_target="tpu_custom_call" | custom-call | flops 6000000000 | bytes 31457280 | tf_op jit(solution)/shard_map/block/pallas_call | solution.py:468
  75.0 2.7 %copy.9 = bf16[1,8,16,6144]{3,2,1,0:T(8,128)(2,1)} copy(bf16[1,8,16,6144]{3,2,1,0:T(8,128)(2,1)} %bitcast.7) | data formatting | bytes 3145728

commit v4 on v3

--- a/solution.py
+++ b/solution.py
@@ -19,6 +19,7 @@
 SHARD = 18
 SHARD_O = 12
 NEG = -1e30
+VERT = ((64, 16), (112, 32), (176, 32), (240, 32), (304, 16))
 
 
 def kernel(
@@ -46,7 +47,7 @@
     yp, ym = dev(0, 1, 0, 0), dev(0, 3, 0, 0)
     zp, zm = dev(0, 0, 1, 0), dev(0, 0, 7, 0)
     ya, yb, za, zb = 4 * cy, 4 * (1 - cy), 8 + 4 * cz, 8 + 4 * (1 - cz)
-    came = [ya + i for i in range(4)] + [za + i for i in range(4)] + [16, 17] + [yb + i for i in range(4)] + [zb + i for i in range(4)]
+    came = [ya + i for i in range(4)] + [za + i for i in range(4)] + [16 + cz, 17 - cz] + [yb + i for i in range(4)] + [zb + i for i in range(4)]
 
     c_qi = pltpu.make_async_copy(qi_any, QI, loc.at[3])
     c_oi = pltpu.make_async_copy(oi_any, OI, loc.at[4])
@@ -77,8 +78,9 @@
 
     def a_forward(j):
         d = a_ref(f_oth, j)
-        to = (yp, ym, zp, zm)[(j // 4) * 2 + j % 2]
-        return rc(d, d, ws.at[10 + j], wr.at[10 + j], to)
+        to = zm if j == 8 else (yp, ym, zp, zm)[(j // 4) * 2 + j % 2]
+        at = 9 if j == 8 else 10 + j
+        return rc(d, d, ws.at[at], wr.at[at], to)
 
     def a_recv(j):
         d = a_ref(f_oth, j)
@@ -92,13 +94,14 @@
         d = a_ref(f_osb, j)
         return rc(d, d, ss.at[j], sr.at[j], sib)
 
-    parts = [cy, 2 + cz, 1 - cy, 2 + 1 - cz]
+    parts = [6 * cy, 12 + 12 * cz, 6 * (1 - cy), 12 + 12 * (1 - cz)]
+    sizes = (6, 12, 6, 12)
 
     def o_ref(f, j):
-        return WO.at[pl.ds(f * 36 + parts[j] * 9, 9)]
+        return WO.at[pl.ds(f * 36 + parts[j], sizes[j])]
 
     def o_first(j):
-        return rc(wo.at[pl.ds(parts[j] * 9, 9)], o_ref(f_own, j), bs.at[j], br.at[j], (xp, xm)[j])
+        return rc(wo.at[pl.ds(parts[j], sizes[j])], o_ref(f_own, j), bs.at[j], br.at[j], (xp, xm)[j])
 
     def o_forward(j):
         d = o_ref(f_oth, j)
@@ -169,8 +172,8 @@
             def _():
                 rc(d, d, hs.at[j], hr.at[j], sib).wait_recv()
 
-    a_starts = [a_first(j) for j in (0, 4, 1, 5, 2, 6, 3, 7, 8, 9)]
-    for c in a_starts:
+    a_starts = [a_first(j) for j in (0, 4, 1, 5, 2, 6, 3, 7, 8)]
+    for c in a_starts[:4]:
         c.start()
     sa_send.start()
 
@@ -232,8 +235,8 @@
             i = QI[j, cb]
             if part == "sides":
                 cols.append(jnp.concatenate([ref[i, 0:64, :], ref[i, 320:384, :]], axis=0))
-            elif part in ("middle", "both"):
-                cols.append(ref[i, 64:320, :])
+            elif part == "vert":
+                cols.append(jnp.concatenate([ref[i, a : a + n, :] for a, n in VERT], axis=0))
             else:
                 cols.append(ref[i])
         return jnp.concatenate(cols, axis=1)
@@ -243,25 +246,30 @@
         return jnp.dot(rows_of(ref, cb, part), w, preferred_element_type=jnp.float32).astype(jnp.bfloat16)
 
     def chunk(lo, count, part):
-        @pl.when(lo < HEADS)
-        def _():
-            if part in ("own", "both", "all"):
+        if part in ("own", "all"):
+            @pl.when(lo < HEADS)
+            def _():
                 for e in range(count):
                     Q[lo + e] = project(NO, lo + e, "own")
 
         @pl.when(lo >= HEADS)
         def _():
-            if part == "own":
-                return
             for e in range(count):
-                r = project(N, lo + e, part)
-                if part in ("middle", "both"):
-                    KV[lo + e - HEADS, 64:320, :] = r
+                at = lo + e - HEADS
+                r = project(NO if part == "own" else N, lo + e, part)
+                if part == "own":
+                    for g in range(4):
+                        KV[at, 64 * g + 80 : 64 * g + 112, :] = r[32 * g : 32 * g + 32]
+                elif part == "vert":
+                    k = 0
+                    for a, n in VERT:
+                        KV[at, a : a + n, :] = r[k : k + n]
+                        k += n
                 elif part == "sides":
-                    KV[lo + e - HEADS, 0:64, :] = r[0:64]
-                    KV[lo + e - HEADS, 320:384, :] = r[64:128]
+                    KV[at, 0:64, :] = r[0:64]
+                    KV[at, 320:384, :] = r[64:128]
                 else:
-                    KV[lo + e - HEADS] = r
+                    KV[at] = r
 
     def shard(f, part):
         def step(c, _):
@@ -349,6 +357,8 @@
     c_tok.wait()
     regroup()
     h_start("NR", "SR", "N", "S", "ND", "SD", "W", "E")
+    for c in a_starts[4:]:
+        c.start()
 
     @pl.when(jnp.logical_not(up))
     def _():
@@ -383,12 +393,12 @@
     pump_x(0)
     make_bias()
     pump_x(1)
+    h_wait("NR", "SR")
+    h_start("NF", "SF")
     c_wq.wait()
     c_qi.wait()
     shard(f_own, "own")
     pump_x(2)
-    h_wait("NR", "SR")
-    h_start("NF", "SF")
     o_starts = [o_first(0), o_first(1)]
     for c in o_starts:
         c.start()
@@ -396,46 +406,55 @@
     sa_recv.wait_recv()
     shard(f_sib, "own")
     pump_x(3)
+    def base(f, j):
+        return f * SHARD + (16 if j == 8 else came[j])
+
+    def received(j, part):
+        chunk(base(f_oth, j), 2, part)
+        for i in range(2):
+            s_recv(j + i).wait_recv()
+        chunk(base(f_osb, j), 2, part)
+
+    for j in (0, 4, 2, 6):
+        received(j, "own")
     h_wait("N", "S", "ND", "SD", "NF", "SF")
     h_start("NW", "NE", "SW", "SE")
     norm_vertical()
-    pump(8, 9, 10, 14)
+    a_recv(8).wait_recv()
+    a_forward(8).start()
+    s_send(8).start()
+    pump(10, 14)
+    shard(f_own, "vert")
+    pump(11, 15, 12, 16)
+    shard(f_sib, "vert")
+    pump(13, 17, 9)
     for j in range(2):
         o_recv(j).wait_recv()
         o_forward(j).start()
         os_send(j).start()
-    shard(f_own, "middle")
-    pump(11, 15, 12, 16)
-    shard(f_sib, "middle")
-    pump(13, 17)
-
-    def received(j, part):
-        chunk(f_oth * SHARD + came[j], 2, part)
-        for i in range(2):
-            s_recv(j + i).wait_recv()
-        chunk(f_osb * SHARD + came[j], 2, part)
-
-    for j in (0, 4, 2, 6, 8):
-        received(j, "both")
+
+    for j in (0, 4, 2, 6):
+        chunk(base(f_oth, j), 2, "vert")
+        chunk(base(f_osb, j), 2, "vert")
     h_wait("W", "E", "NW", "NE", "SW", "SE")
     norm_sides()
     shard(f_own, "sides")
     shard(f_sib, "sides")
-    for j in (0, 4, 2, 6, 8):
-        chunk(f_oth * SHARD + came[j], 2, "sides")
-        chunk(f_osb * SHARD + came[j], 2, "sides")
-    for j in (10, 14, 12, 16):
+    for j in (0, 4, 2, 6):
+        chunk(base(f_oth, j), 2, "sides")
+        chunk(base(f_osb, j), 2, "sides")
+    for j in (8, 10, 14, 12, 16):
         received(j, "all")
 
     def head(i, _):
         attend(3 * i, 3)
         return 0
 
-    lax.fori_loop(0, HEADS // 3, head, 0)
-
+    lax.fori_loop(0, HEADS // 6, head, 0)
     for j in range(2, 4):
         o_recv(j).wait_recv()
         os_send(j).start()
+    lax.fori_loop(HEADS // 6, HEADS // 3, head, 0)
     c_wo.wait()
     c_oi.wait()
     sb_recv.wait_recv()
@@ -450,7 +469,7 @@
 
     for c in a_starts + o_starts + [sa_send, sb_send]:
         c.wait_send()
-    for j in range(8):
+    for j in range(9):
         a_forward(j).wait_send()
     for j in range(2):
         o_forward(j).wait_send()

time: 77.9 us -> 78.1 us (level)
  the two profiles are of different devices: /device:TPU:27 before, /device:TPU:101 now
where the time goes in v4:
time: 78.1 us; the launch traced here: 77.9 us
  Pallas kernels  75.2 us (96%)
  local copies, waits for them, and re-layouts  2.69 us (3%)
    pallas_call x1, Pallas kernels, body(): pl.pallas_call(kernel, out_shape=jax.ShapeDtypeStruct((OWN, 6144), bf), i...  75.2 us
    unnamed x1, local copies, waits for them, and re-layouts  2.69 us

profile of v4, /device:TPU:101, one launch (start us, length us, event | category | flops | bytes accessed | tf_op | source)
XLA Modules:
  0.0 77.9 jit_solution(763850883255288067)
XLA Ops:
  0.0 75.2 %block.1 = bf16[128,6144]{1,0:T(8,128)(2,1)} custom-call(s32[6,72]{1,0:T(8,128)} %bitcast.12, s32[3,48]{1,0:T(4,128)} %bitcast.13, bf16[128,6144]{1,0:T(8,128)(2,1)} %bitcast.9, f32[1,6144]{1,0:T(1,128)} %bitcast.11, f32[24,81]{1,0:T(8,128)} %rel.1, bf16[108,128,128]{2,1,0:T(8,128)(2,1)} %bitcast.8, bf16[36,128,128]{2,1,0:T(8,128)(2,1)} %bitcast.10), custom_call_target="tpu_custom_call" | custom-call | flops 6000000000 | bytes 31457280 | tf_op jit(solution)/shard_map/block/pallas_call | solution.py:487
  75.2 2.7 %copy.9 = bf16[1,8,16,6144]{3,2,1,0:T(8,128)(2,1)} copy(bf16[1,8,16,6144]{3,2,1,0:T(8,128)(2,1)} %bitcast.7) | data formatting | bytes 3145728

commit v5 on v4

--- a/solution.py
+++ b/solution.py
@@ -19,6 +19,7 @@
 SHARD = 18
 SHARD_O = 12
 NEG = -1e30
+CORNERS = (0, 48, 320, 368)
 VERT = ((64, 16), (112, 32), (176, 32), (240, 32), (304, 16))
 
 
@@ -222,19 +223,28 @@
 
         lax.fori_loop(0, 8, step, 0)
 
-    def norm_sides():
+    def norm_edges():
         def step(i, _):
-            norm_rows(5 * (i // 4), pl.multiple_of(16 * (i % 4), 16))
+            norm_rows(5 * (i // 2), pl.multiple_of(16 + 16 * (i % 2), 16), pl.multiple_of(OWN + 16 * i, 16))
             return 0
 
-        lax.fori_loop(0, 8, step, 0)
+        lax.fori_loop(0, 4, step, 0)
+
+    def norm_corners():
+        def step(i, _):
+            norm_rows(5 * (i // 2), pl.multiple_of(48 * (i % 2), 16))
+            return 0
+
+        lax.fori_loop(0, 4, step, 0)
 
     def rows_of(ref, cb, part):
         cols = []
         for j in range(KEEP):
             i = QI[j, cb]
-            if part == "sides":
-                cols.append(jnp.concatenate([ref[i, 0:64, :], ref[i, 320:384, :]], axis=0))
+            if part == "q":
+                cols.append(ref[i, 0:OWN, :])
+            elif part == "corners":
+                cols.append(jnp.concatenate([ref[i, a : a + 16, :] for a in CORNERS], axis=0))
             elif part == "vert":
                 cols.append(jnp.concatenate([ref[i, a : a + n, :] for a, n in VERT], axis=0))
             else:
@@ -250,7 +260,7 @@
             @pl.when(lo < HEADS)
             def _():
                 for e in range(count):
-                    Q[lo + e] = project(NO, lo + e, "own")
+                    Q[lo + e] = project(NO, lo + e, "q")
 
         @pl.when(lo >= HEADS)
         def _():
@@ -260,14 +270,16 @@
                 if part == "own":
                     for g in range(4):
                         KV[at, 64 * g + 80 : 64 * g + 112, :] = r[32 * g : 32 * g + 32]
+                    KV[at, 16:48, :] = r[128:160]
+                    KV[at, 336:368, :] = r[160:192]
                 elif part == "vert":
                     k = 0
                     for a, n in VERT:
                         KV[at, a : a + n, :] = r[k : k + n]
                         k += n
-                elif part == "sides":
-                    KV[at, 0:64, :] = r[0:64]
-                    KV[at, 320:384, :] = r[64:128]
+                elif part == "corners":
+                    for k, a in enumerate(CORNERS):
+                        KV[at, a : a + 16, :] = r[16 * k : 16 * k + 16]
                 else:
                     KV[at] = r
 
@@ -395,6 +407,8 @@
     pump_x(1)
     h_wait("NR", "SR")
     h_start("NF", "SF")
+    h_wait("W", "E")
+    norm_edges()
     c_wq.wait()
     c_qi.wait()
     shard(f_own, "own")
@@ -436,13 +450,13 @@
     for j in (0, 4, 2, 6):
         chunk(base(f_oth, j), 2, "vert")
         chunk(base(f_osb, j), 2, "vert")
-    h_wait("W", "E", "NW", "NE", "SW", "SE")
-    norm_sides()
-    shard(f_own, "sides")
-    shard(f_sib, "sides")
+    h_wait("NW", "NE", "SW", "SE")
+    norm_corners()
+    shard(f_own, "corners")
+    shard(f_sib, "corners")
     for j in (0, 4, 2, 6):
-        chunk(base(f_oth, j), 2, "sides")
-        chunk(base(f_osb, j), 2, "sides")
+        chunk(base(f_oth, j), 2, "corners")
+        chunk(base(f_osb, j), 2, "corners")
     for j in (8, 10, 14, 12, 16):
         received(j, "all")
 
@@ -493,7 +507,7 @@
             pltpu.VMEM((OWN, 6144), bf),
             pltpu.VMEM((6, 64, 6144), bf),
             pltpu.VMEM((GROUPS, ALL, HD), bf),
-            pltpu.VMEM((GROUPS, OWN, HD), bf),
+            pltpu.VMEM((GROUPS, OWN + 64, HD), bf),
             pltpu.VMEM((432, HD, HD), bf),
             pltpu.VMEM((144, HD, HD), bf),
             pltpu.VMEM((HEADS, OWN, HD), bf),

time: 78.1 us -> 76 us (0.973)
  Pallas kernels: 75.2 us -> 73.2 us
    pallas_call x1, Pallas kernels: 75.2 us -> 73.2 us  [body(): pl.pallas_call(kernel, out_shape=jax.ShapeDtypeStruct((OWN, 6144), bf), i...]
where the time goes in v5:
time: 76 us; the launch traced here: 75.9 us
  Pallas kernels  73.2 us (96%)
  local copies, waits for them, and re-layouts  2.69 us (4%)
    pallas_call x1, Pallas kernels, body(): pl.pallas_call(kernel, out_shape=jax.ShapeDtypeStruct((OWN, 6144), bf), i...  73.2 us
    unnamed x1, local copies, waits for them, and re-layouts  2.69 us

profile of v5, /device:TPU:101, one launch (start us, length us, event | category | flops | bytes accessed | tf_op | source)
XLA Modules:
  0.0 75.9 jit_solution(1046522292758744560)
XLA Ops:
  0.0 73.2 %block.1 = bf16[128,6144]{1,0:T(8,128)(2,1)} custom-call(s32[6,72]{1,0:T(8,128)} %bitcast.12, s32[3,48]{1,0:T(4,128)} %bitcast.13, bf16[128,6144]{1,0:T(8,128)(2,1)} %bitcast.9, f32[1,6144]{1,0:T(1,128)} %bitcast.11, f32[24,81]{1,0:T(8,128)} %rel.1, bf16[108,128,128]{2,1,0:T(8,128)(2,1)} %bitcast.8, bf16[36,128,128]{2,1,0:T(8,128)(2,1)} %bitcast.10), custom_call_target="tpu_custom_call" | custom-call | flops 6000000000 | bytes 31457280 | tf_op jit(solution)/shard_map/block/pallas_call | solution.py:501
  73.2 2.7 %copy.9 = bf16[1,8,16,6144]{3,2,1,0:T(8,128)(2,1)} copy(bf16[1,8,16,6144]{3,2,1,0:T(8,128)(2,1)} %bitcast.7) | data formatting | bytes 3145728
